TPU v7x, 512 devices: a whole 4x4x16 slice. The times are simulated.
512 devices in a mesh: rec: 8 (over y, core), tm: 64 (over x, z).
Axes of the slice: x: 4, y: 4, z: 16, core: 2. Of those that a mesh axis runs over, the one named last changes fastest.
Arguments:
- summary: bfloat16 [8, 64, 1024, 1024], P('rec', 'tm'), as said below
- guess: bfloat16 [8, 16384, 1024], P('rec', 'tm'), may hold values from 0.099609375 to 3
- emission: bfloat16 [8, 16384, 1024], P('rec', 'tm'), may hold values from 0.049804688 to 1
- transition: bfloat16 [1024, 1024], P(None, 'rec'), as said below
- start: bfloat16 [8, 1024], P('rec'), may hold values from 0.099609375 to 3
Outputs:
- combined: bfloat16 [8, 32768, 1024], P('rec', 'tm')
- level_loglik: float32 [8], P('rec')
- forward: bfloat16 [8, 16384, 1024], P('rec', 'tm')
- frame_logscale: float32 [8, 16384], P('rec', 'tm')
Inputs may be any that keep to these rules, and one draw needn't show every extreme that they name: `summary`: every entry is positive. `transition`: every entry is positive.
All inputs are finite; a program needn't handle non-finite values.
Results may differ from a plain program's by a relative error of at most 0.0052.
Values may be sent and summed in bfloat16 or wider, within the bound.
No kernel may reach another device: no remote copies, remote signals or barrier semaphores. Data moves between devices by JAX's collectives and lax.ppermute only.
A program may use at most 64 MiB of HBM per device.

v0:
```python
import jax
import jax.numpy as jnp
from jax import lax
from jax.sharding import PartitionSpec as P

SWEEPS = 4


def swapped(block, axis, stride):
    count = lax.axis_size(axis)
    route = []
    for low in range(count):
        high = low | 1 << stride
        if high != low and high < count:
            route += [(low, high), (high, low)]
    return lax.ppermute(block, axis, route)


def from_behind(x, axis, by):
    size = lax.axis_size(axis)
    pairs = [(i, i + by) for i in range(size) if 0 <= i + by < size]
    return lax.ppermute(x, axis, pairs)


def local(summary, guess, emission, transition, start):
    mine_tile = summary[0, 0]
    states = mine_tile.shape[0]
    half_rows = states // 2
    parity = lax.axis_index("tm") % 2
    partner = swapped(mine_tile, "tm", 0)
    first_tile = jnp.where(parity == 0, mine_tile, partner)
    second_tile = jnp.where(parity == 0, partner, mine_tile)
    left_part = lax.dynamic_slice_in_dim(first_tile, parity * half_rows, half_rows, 0)
    product = jnp.dot(left_part, second_tile, preferred_element_type=jnp.float32)
    half_total = jnp.sum(product).reshape(1)
    pair_total = half_total + swapped(half_total, "tm", 0)
    level_loglik = lax.psum(0.5 * jnp.log(pair_total / states), "tm") / (lax.axis_size("tm") // 2)
    combined = (product * (states * states / pair_total[0])).astype(jnp.bfloat16)[None]
    columns = lax.all_gather(transition, "rec", axis=1, tiled=True)
    forward_rows = guess[0]
    emit_rows = emission[0]
    frame_count = forward_rows.shape[0]
    at_start = lax.axis_index("tm") == 0
    row_mean = jnp.ones((frame_count, 1), jnp.float32)
    for sweep_index in range(SWEEPS):
        left_row = from_behind(forward_rows[-1:], "tm", 1)
        first_row = jnp.where(at_start, start, left_row)
        prior_rows = jnp.concatenate([first_row, forward_rows[:-1]], axis=0)
        unscaled = jnp.dot(prior_rows, columns, preferred_element_type=jnp.float32) * emit_rows
        row_mean = jnp.mean(unscaled, axis=1, keepdims=True)
        forward_rows = (unscaled / row_mean).astype(jnp.bfloat16)
    frame_logscale = jnp.log(row_mean[:, 0])[None]
    return (combined, level_loglik, forward_rows[None], frame_logscale)


def solution(mesh):
    return jax.shard_map(
        local,
        mesh=mesh,
        in_specs=(
            P("rec", "tm", None, None),
            P("rec", "tm", None),
            P("rec", "tm", None),
            P(None, "rec"),
            P("rec", None),
        ),
        out_specs=(P("rec", "tm", None), P("rec"), P("rec", "tm", None), P("rec", "tm")),
        check_vma=False,
    )
```

profile of v0, /device:TPU:16, one launch (start us, length us, event | category | flops | bytes accessed | tf_op | source)
XLA Modules:
  0.0 238.9 jit_solution(16517027923723144678)
XLA Ops:
  7.2 0.7 all-gather.2.cloned.1.call-update
  7.9 0.7 slice_bitcast_fusion.1
  8.6 3.8 %collective-permute-start.2 = (bf16[1,1024]{1,0:T(2,128)(2,1)S(1)}, bf16[1,1024]{1,0:T(2,128)(2,1)S(1)}, u32[]{:S(2)}, u32[]{:S(2)}) collective-permute-start(bf16[1,1024]{1,0:T(2,128)(2,1)S(1)} %slice_bitcast_fusion.1), channel_id=1, source_target_pairs={{0,1},{1,2},{2,3},{3,4},{4,5},{5,6},{6,7},{7,8},{8,9},{9,10},{10,1... | collective-permute-start | bytes 6152 | tf_op jit(solution)/shard_map/ppermute | solution.py:22
  12.4 3.8 %collective-permute-start = (bf16[1024,1024]{1,0:T(8,128)(2,1)}, bf16[1024,1024]{1,0:T(8,128)(2,1)}, u32[]{:S(2)}, u32[]{:S(2)}) collective-permute-start(bf16[1024,1024]{1,0:T(8,128)(2,1)} %bitcast.29), channel_id=1, source_target_pairs={{0,1},{1,0},{2,3},{3,2},{4,5},{5,4},{6,7},{7,6},{8,9},{9,8},{10,11... | collective-permute-start | bytes 6291464 | tf_op jit(solution)/shard_map/ppermute | solution.py:16
  16.3 1.1 slice_bitcast_fusion
  17.4 0.7 broadcast_select_fusion.3
  18.1 31.0 %all-gather.2.cloned.1.call-done = bf16[1024,1024]{1,0:T(8,128)(2,1)} async-done(((bf16[1024,128]{1,0:T(8,128)(2,1)}), bf16[1024,1024]{1,0:T(8,128)(2,1)}) %all-gather.2.cloned.1.call-update) | async-done | bytes 2097168 | tf_op jit(solution)/shard_map/all_gather | solution.py:39
  49.1 2.6 %fusion.26 = (f32[256]{0:T(256)S(1)}, f32[256,1024]{1,0:T(8,128)S(1)}) fusion(bf16[1,256,1024]{2,1,0:T(8,128)(2,1)} %param.7, bf16[1024,1024]{1,0:T(8,128)(2,1)} %all-gather.2.cloned.1.call-done, bf16[255,1024]{1,0:T(8,128)(2,1)S(1)} %slice_bitcast_fusion, bf16[1,1024]{1,0:T(2,128)(2,1)S(1)} %broadcast_select_fusion.3), kind=kOutput, calls=%fused_computation.46 | convolution fusion | flops 538705664 | bytes 4195328 | tf_op jit(solution)/shard_map/dot_general | solution.py:49
  51.7 0.2 divide_convert_fusion.3
  51.9 3.5 %collective-permute-start.3 = (bf16[1,1024]{1,0:T(2,128)(2,1)S(1)}, bf16[1,1024]{1,0:T(2,128)(2,1)S(1)}, u32[]{:S(2)}, u32[]{:S(2)}) collective-permute-start(bf16[1,1024]{1,0:T(2,128)(2,1)S(1)} %slice.40), channel_id=1, source_target_pairs={{0,1},{1,2},{2,3},{3,4},{4,5},{5,6},{6,7},{7,8},{8,9},{9,10},{10,1... | collective-permute-start | bytes 6152 | tf_op jit(solution)/shard_map/ppermute | solution.py:22
  55.4 5.8 %collective-permute-done.3 = bf16[1,1024]{1,0:T(2,128)(2,1)S(1)} collective-permute-done((bf16[1,1024]{1,0:T(2,128)(2,1)S(1)}, bf16[1,1024]{1,0:T(2,128)(2,1)S(1)}, u32[]{:S(2)}, u32[]{:S(2)}) %collective-permute-start.3) | collective-permute-done | bytes 2080 | tf_op jit(solution)/shard_map/ppermute | solution.py:22
  61.3 0.8 fusion.27
  62.3 4.4 %collective-permute-start.4 = (bf16[1,1024]{1,0:T(2,128)(2,1)S(1)}, bf16[1,1024]{1,0:T(2,128)(2,1)S(1)}, u32[]{:S(2)}, u32[]{:S(2)}) collective-permute-start(bf16[1,1024]{1,0:T(2,128)(2,1)S(1)} %slice.42), channel_id=1, source_target_pairs={{0,1},{1,2},{2,3},{3,4},{4,5},{5,6},{6,7},{7,8},{8,9},{9,10},{10,1... | collective-permute-start | bytes 6152 | tf_op jit(solution)/shard_map/ppermute | solution.py:22
  66.7 4.0 %fusion.25 = (f32[]{:T(128)}, f32[512,1024]{1,0:T(8,128)S(1)}) fusion(bf16[1024,1024]{1,0:T(8,128)(2,1)} %collective-permute-done, bf16[1024,1024]{1,0:T(8,128)(2,1)S(1)} %bitcast.30, pred[]{:T(512)S(6)} %eq.9, s32[]{:T(128)S(6)} %select_n.45), kind=kOutput, calls=%fused_computation.45 | convolution fusion | flops 1075838976 | bytes 8390148 | tf_op jit(solution)/shard_map/dot_general | solution.py:34
  70.7 3.8 %collective-permute-start.1 = (f32[1]{0:T(128)}, f32[1]{0:T(128)}, u32[]{:S(2)}, u32[]{:S(2)}) collective-permute-start(f32[1]{0:T(128)} %bitcast.1), channel_id=1, source_target_pairs={{0,1},{1,0},{2,3},{3,2},{4,5},{5,4},{6,7},{7,6},{8,9},{9,8},{10,11... | collective-permute-start | bytes 20 | tf_op jit(solution)/shard_map/ppermute | solution.py:16
  74.5 1.9 collective-permute-done.1
  77.7 0.8 fusion.28
  78.6 0.2 divide_convert_fusion.1
  78.7 3.8 %collective-permute-start.5 = (bf16[1,1024]{1,0:T(2,128)(2,1)S(1)}, bf16[1,1024]{1,0:T(2,128)(2,1)S(1)}, u32[]{:S(2)}, u32[]{:S(2)}) collective-permute-start(bf16[1,1024]{1,0:T(2,128)(2,1)S(1)} %slice.44), channel_id=1, source_target_pairs={{0,1},{1,2},{2,3},{3,4},{4,5},{5,6},{6,7},{7,8},{8,9},{9,10},{10,1... | collective-permute-start | bytes 6152 | tf_op jit(solution)/shard_map/ppermute | solution.py:22
  82.5 1.2 fusion.3
  83.7 144.1 %psum.7 = f32[1]{0:T(128)} all-reduce(f32[1]{0:T(128)S(6)} %mul.27), channel_id=1, replica_groups=mesh['rec'=8,'tm'=64] {'tm'}, use_global_device_ids=true, to_apply=%region_1.2 | all-reduce | flops 1 | bytes 8 | tf_op jit(solution)/shard_map/psum | solution.py:37
  228.5 0.8 fusion.29
  229.4 0.6 fusion.24
  229.9 0.9 fusion.18
  (23 shorter events, 0.3 us)
Async XLA Ops:
  7.2 41.9 %all-gather.2.cloned.1.call-start = ((), (), s32[]{:S(2)}) async-start(), calls=%async_computation | async-start | bytes 2359296 | tf_op jit(solution)/shard_map/all_gather | solution.py:39
  8.6 8.7 %collective-permute-start.2 = (bf16[1,1024]{1,0:T(2,128)(2,1)S(1)}, bf16[1,1024]{1,0:T(2,128)(2,1)S(1)}, u32[]{:S(2)}, u32[]{:S(2)}) collective-permute-start(bf16[1,1024]{1,0:T(2,128)(2,1)S(1)} %slice_bitcast_fusion.1), channel_id=1, source_target_pairs={{0,1},{1,2},{2,3},{3,4},{4,5},{5,6},{6,7},{7,8},{8,9},{9,10},{10,1... | collective-permute-start | bytes 6152 | tf_op jit(solution)/shard_map/ppermute | solution.py:22
  12.4 54.2 %collective-permute-start = (bf16[1024,1024]{1,0:T(8,128)(2,1)}, bf16[1024,1024]{1,0:T(8,128)(2,1)}, u32[]{:S(2)}, u32[]{:S(2)}) collective-permute-start(bf16[1024,1024]{1,0:T(8,128)(2,1)} %bitcast.29), channel_id=1, source_target_pairs={{0,1},{1,0},{2,3},{3,2},{4,5},{5,4},{6,7},{7,6},{8,9},{9,8},{10,11... | collective-permute-start | bytes 6291464 | tf_op jit(solution)/shard_map/ppermute | solution.py:16
  18.1 43.1 %copy-start = (bf16[1,1024]{1,0:T(2,128)(2,1)S(1)}, bf16[1,1024]{1,0:T(2,128)(2,1)}, u32[]{:S(2)}) copy-start(bf16[1,1024]{1,0:T(2,128)(2,1)} %param.9) | copy-start | bytes 6148
  18.1 43.1 %copy-start.3 = (bf16[1,256,1024]{2,1,0:T(8,128)(2,1)S(1)}, bf16[1,256,1024]{2,1,0:T(8,128)(2,1)}, u32[]{:S(2)}) copy-start(bf16[1,256,1024]{2,1,0:T(8,128)(2,1)} %param.7) | copy-start | bytes 1572868
  49.1 12.2 %copy-start.2 = (bf16[1024,1024]{1,0:T(8,128)(2,1)S(1)}, bf16[1024,1024]{1,0:T(8,128)(2,1)}, u32[]{:S(2)}) copy-start(bf16[1024,1024]{1,0:T(8,128)(2,1)} %all-gather.2.cloned.1.call-done) | copy-start | bytes 6291460
  51.9 9.3 %collective-permute-start.3 = (bf16[1,1024]{1,0:T(2,128)(2,1)S(1)}, bf16[1,1024]{1,0:T(2,128)(2,1)S(1)}, u32[]{:S(2)}, u32[]{:S(2)}) collective-permute-start(bf16[1,1024]{1,0:T(2,128)(2,1)S(1)} %slice.40), channel_id=1, source_target_pairs={{0,1},{1,2},{2,3},{3,4},{4,5},{5,6},{6,7},{7,8},{8,9},{9,10},{10,1... | collective-permute-start | bytes 6152 | tf_op jit(solution)/shard_map/ppermute | solution.py:22
  61.3 5.4 %copy-start.1 = (bf16[1,1,1024,1024]{3,2,1,0:T(8,128)(2,1)S(1)}, bf16[1,1,1024,1024]{3,2,1,0:T(8,128)(2,1)}, u32[]{:S(2)}) copy-start(bf16[1,1,1024,1024]{3,2,1,0:T(8,128)(2,1)} %param.5) | copy-start | bytes 6291460
  62.3 15.4 %collective-permute-start.4 = (bf16[1,1024]{1,0:T(2,128)(2,1)S(1)}, bf16[1,1024]{1,0:T(2,128)(2,1)S(1)}, u32[]{:S(2)}, u32[]{:S(2)}) collective-permute-start(bf16[1,1024]{1,0:T(2,128)(2,1)S(1)} %slice.42), channel_id=1, source_target_pairs={{0,1},{1,2},{2,3},{3,4},{4,5},{5,6},{6,7},{7,8},{8,9},{9,10},{10,1... | collective-permute-start | bytes 6152 | tf_op jit(solution)/shard_map/ppermute | solution.py:22
  70.7 5.7 %collective-permute-start.1 = (f32[1]{0:T(128)}, f32[1]{0:T(128)}, u32[]{:S(2)}, u32[]{:S(2)}) collective-permute-start(f32[1]{0:T(128)} %bitcast.1), channel_id=1, source_target_pairs={{0,1},{1,0},{2,3},{3,2},{4,5},{5,4},{6,7},{7,6},{8,9},{9,8},{10,11... | collective-permute-start | bytes 20 | tf_op jit(solution)/shard_map/ppermute | solution.py:16
  78.7 149.8 %collective-permute-start.5 = (bf16[1,1024]{1,0:T(2,128)(2,1)S(1)}, bf16[1,1024]{1,0:T(2,128)(2,1)S(1)}, u32[]{:S(2)}, u32[]{:S(2)}) collective-permute-start(bf16[1,1024]{1,0:T(2,128)(2,1)S(1)} %slice.44), channel_id=1, source_target_pairs={{0,1},{1,2},{2,3},{3,4},{4,5},{5,6},{6,7},{7,8},{8,9},{9,10},{10,1... | collective-permute-start | bytes 6152 | tf_op jit(solution)/shard_map/ppermute | solution.py:22
Sparse Core Ops, SparseCore 0:
  10.1 38.9 all-gather.1
where the time goes:
time: 239 us
  blocking collectives  144 us (60%)
  waiting for transfers between devices  39.4 us (16%)
  starting transfers between devices  23 us (10%)
  between operations  17.4 us (7%)
  matrix products  9.05 us (4%)
  other arithmetic  4 us (2%)
    psum x1, blocking collectives, local(): lax.psum(0.5 * jnp.log(pair_total / states), 'tm')  144 us
    all_gather x1, waiting for transfers between devices, local(): columns = lax.all_gather(transition, 'rec', axis=1, tiled=True)  31 us
    ppermute x4, starting transfers between devices, from_behind(): return lax.ppermute(x, axis, pairs)  15.4 us
    ppermute x2, starting transfers between devices, swapped(): return lax.ppermute(block, axis, route)  7.59 us
    ppermute x4, waiting for transfers between devices, from_behind(): return lax.ppermute(x, axis, pairs)  5.84 us
    dot_general x4, matrix products, local(): jnp.dot(prior_rows, columns, preferred_element_type=jnp.float32) * emit_rows  5.05 us
  transfers between devices with their start and end apart: 7, of which 3 were waited for; matrix products, arithmetic and copies ran while one was open for 5% of the time, Pallas kernels for 0%

commit v1 on v0

v1 whole, which is shorter than its diff:
```python
import functools

import jax
import jax.numpy as jnp
from jax import lax
from jax.experimental import pallas as pl
from jax.experimental.pallas import tpu as pltpu
from jax.sharding import PartitionSpec as P

SWEEPS = 4
EDGE = 16
F32 = jnp.float32
BF16 = jnp.bfloat16
VMEM = pltpu.VMEM
HBM = pltpu.HBM
LIGHT = pl.CostEstimate(flops=1, bytes_accessed=1, transcendentals=0)


def parity():
    return lax.rem(lax.axis_index("tm"), 2)


def params(mib=24):
    return pltpu.CompilerParams(vmem_limit_bytes=mib * 1024 * 1024)


def matmul(a, b):
    return jnp.dot(a, b, preferred_element_type=F32)


def edge_kernel(sums, guess, emit, order, out):
    row = lax.broadcasted_iota(jnp.int32, out.shape, 0)
    rows = pltpu.roll(guess[...].astype(F32)[8:], 5, 0)
    out[...] = jnp.where(row == 0, sums[...], jnp.where(row < 5, rows, emit[...].astype(F32)[8:]))


def edge_after(sums, guess_rows, emit_rows, order):
    states = guess_rows.shape[1]
    last = guess_rows.shape[0] // EDGE - 1
    tail = pl.BlockSpec((EDGE, states), lambda i: (last, 0))
    return pl.pallas_call(
        edge_kernel,
        grid=(1,),
        in_specs=[pl.BlockSpec((1, states), lambda i: (0, 0)), tail, tail, pl.BlockSpec(memory_space=pl.ANY)],
        out_specs=pl.BlockSpec((8, states), lambda i: (0, 0)),
        out_shape=jax.ShapeDtypeStruct((8, states), F32),
        compiler_params=params(),
        cost_estimate=LIGHT,
        name="edge",
    )(sums, guess_rows, emit_rows, order)


def total_kernel(column_sums, row_sums, mine, logs, again):
    states = mine.shape[1]
    value = jnp.sum(column_sums[...] * row_sums[...], axis=1, keepdims=True)
    logs[...] = jnp.broadcast_to(jnp.log(value * (1.0 / states)), logs.shape)
    again[...] = mine[...]


def log_total(column_sums, row_sums, mine, peers):
    return pl.pallas_call(
        total_kernel,
        out_shape=(jax.ShapeDtypeStruct((peers, 128), F32), jax.ShapeDtypeStruct(mine.shape, F32)),
        compiler_params=params(),
        cost_estimate=LIGHT,
        name="log_total",
    )(column_sums, row_sums, mine)


def rows_kernel(first, tile, order, out):
    out[...] = tile[first:, :]


def rows_after(tile, first, order):
    rows, states = tile.shape
    return pl.pallas_call(
        functools.partial(rows_kernel, first),
        in_specs=[pl.BlockSpec(memory_space=VMEM), pl.BlockSpec(memory_space=pl.ANY)],
        out_shape=jax.ShapeDtypeStruct((rows - first, states), BF16),
        compiler_params=params(),
        cost_estimate=LIGHT,
        name="rows",
    )(tile, order)


def sweep_kernel(before, guess, emit, start, columns, others, order, out, logscale, held, table):
    blocks, states, width = columns.shape
    frames = guess.shape[0]
    first = lax.axis_index("tm") == 0
    edge = before[...]
    blank = jnp.zeros_like(edge)
    rows = frames + EDGE
    lead = SWEEPS
    prior = jnp.concatenate([blank, pltpu.roll(edge, 3, 0), guess[...].astype(F32)], axis=0)
    prior = pltpu.roll(prior, rows - (EDGE - lead), 0)
    emission = jnp.concatenate([blank, edge, emit[...].astype(F32)], axis=0)
    row = lax.broadcasted_iota(jnp.int32, (rows, 1), 0)
    start_row = start[...].astype(F32)
    held[...] = jnp.where(jnp.logical_and(first, row == lead - 1), start_row, prior).astype(BF16)
    core = lax.rem(lax.axis_index("rec"), 2)

    def fill(ref, place):
        for b in range(blocks):
            at = (2 * b + place) * width
            table[:, at : at + width] = ref[b]

    @pl.when(core == 0)
    def _():
        fill(columns, 0)
        fill(others, 1)

    @pl.when(core == 1)
    def _():
        fill(columns, 1)
        fill(others, 0)

    for m in range(1, SWEEPS + 1):
        now = rows if m < SWEEPS else frames
        shifted = pltpu.roll(emission, rows - (EDGE - lead + m), 0)[:now]
        unscaled = []
        for b in range(blocks):
            where = slice(2 * b * width, 2 * (b + 1) * width)
            unscaled.append(matmul(held[:now, :], table[:, where]) * shifted[:, where])
        mean = sum(jnp.sum(u, axis=1, keepdims=True) for u in unscaled) * (1.0 / states)
        inverse = 1.0 / mean
        for b, u in enumerate(unscaled):
            where = slice(2 * b * width, 2 * (b + 1) * width)
            scaled = u * inverse
            if m < SWEEPS:
                fixed = jnp.logical_and(first, row == lead - 1 - m)
                held[:, where] = jnp.where(fixed, start_row[:, where], scaled).astype(BF16)
            else:
                out[:, where] = scaled.astype(BF16)
        if m == SWEEPS:
            logscale[...] = jnp.transpose(jnp.broadcast_to(jnp.log(mean), (frames, 128)))[0:1, :]


def sweeps(before, guess, emit, start, columns, others, order):
    frames, states = guess.shape
    return pl.pallas_call(
        sweep_kernel,
        in_specs=[pl.BlockSpec(memory_space=VMEM)] * 6 + [pl.BlockSpec(memory_space=pl.ANY)],
        out_shape=(jax.ShapeDtypeStruct((frames, states), BF16), jax.ShapeDtypeStruct((1, frames), F32)),
        scratch_shapes=[VMEM((frames + EDGE, states), BF16), VMEM((states, states), BF16)],
        compiler_params=params(),
        cost_estimate=LIGHT,
        name="sweeps",
    )(before, guess, emit, start, columns, others, order)


def store_product(left, rights, scale, out, result, out_sems):
    parts, _, width = result.shape
    stores = []
    for p in range(parts):
        where = slice(p * width, (p + 1) * width)
        block = sum(matmul(left[:, first : first + ref.shape[0]], ref[:, where]) for first, ref in rights)
        result[p] = (block * scale).astype(BF16)
        stores.append(pltpu.make_async_copy(result.at[p], out.at[:, pl.ds(p * width, width)], out_sems.at[p]))
        stores[-1].start()
    for store in stores:
        store.wait()


def odd_kernel(own, lower, row_sums, before, out, result, out_sems):
    states = own.shape[0]

    @pl.when(parity() == 1)
    def _():
        scale = (states * states) / jnp.sum(row_sums[...] * before[0:1], axis=1, keepdims=True)
        store_product(lower[...], [(0, own)], scale, out, result, out_sems)


def even_kernel(own, got, column_sums, sums_got, other, order, out, result, out_sems):
    states = own.shape[0]

    @pl.when(parity() == 0)
    def _():
        scale = (states * states) / jnp.sum(column_sums[...] * sums_got[...], axis=1, keepdims=True)
        store_product(own[: states // 2, :], [(0, got)], scale, out, result, out_sems)


def product_call(kernel, name, cost, operands, aliased=None, order=()):
    states = operands[0].shape[0]
    half, parts = states // 2, 4
    specs = [pl.BlockSpec(memory_space=VMEM)] * len(operands)
    if aliased is not None:
        specs.append(pl.BlockSpec(memory_space=HBM))
        operands = operands + [aliased]
    return pl.pallas_call(
        kernel,
        in_specs=specs + [pl.BlockSpec(memory_space=pl.ANY)] * len(order),
        out_specs=pl.BlockSpec(memory_space=HBM),
        out_shape=jax.ShapeDtypeStruct((half, states), BF16),
        scratch_shapes=[VMEM((parts, half, states // parts), BF16), pltpu.SemaphoreType.DMA((parts,))],
        input_output_aliases={} if aliased is None else {len(operands) - 1: 0},
        compiler_params=params(),
        cost_estimate=cost,
        name=name,
    )(*operands, *order)


def mean_kernel(logs, order, level):
    level[...] = jnp.sum(logs[...], axis=0, keepdims=True) * (1.0 / logs.shape[0])


def mean_after(logs, order):
    return pl.pallas_call(
        mean_kernel,
        in_specs=[pl.BlockSpec(memory_space=VMEM), pl.BlockSpec(memory_space=pl.ANY)],
        out_shape=jax.ShapeDtypeStruct((1, 128), F32),
        compiler_params=params(),
        cost_estimate=LIGHT,
        name="mean_log",
    )(logs, order)


def local(summary, guess, emission, transition, start):
    tile = summary[0, 0]
    states = tile.shape[0]
    size, recs = lax.axis_size("tm"), lax.axis_size("rec")
    even = lax.axis_index("tm") % 2 == 0
    back = [(t, t - 1) for t in range(1, size, 2)]
    over = [(t, t + 1) for t in range(0, size, 2)]
    planes = size // 4
    peers = [[r * size + t for t in range(0, size, 2)] for r in range(recs)]
    peers += [[r * size + t for r in range(recs) for t in range(z, size, planes)] for z in range(1, planes, 2)]
    cores = [list(range(c, recs, 2)) for c in range(2)]

    got = lax.ppermute(tile, "tm", back)
    copies = jnp.broadcast_to(transition[None], (recs // 2,) + transition.shape)
    columns = lax.all_to_all(copies, "rec", 0, 0, tiled=True, axis_index_groups=cores)
    wide = tile.astype(F32)
    column_sums, row_sums = jnp.sum(wide, axis=0)[None], jnp.sum(wide, axis=1)[None]
    pair_columns = lax.ppermute(column_sums, "tm", [(t, (t + 2) % size) for t in range(0, size, 2)])
    pair_rows = lax.ppermute(row_sums, "tm", [(t, (t + 1) % size) for t in range(1, size, 2)])
    logs, row_sums_again = log_total(pair_columns, pair_rows, row_sums, size // 2)
    lower = lax.ppermute(rows_after(tile, states // 2, logs), "tm", over)
    all_logs = lax.all_to_all(logs, ("rec", "tm"), 0, 0, tiled=True, axis_index_groups=peers)
    others = lax.ppermute(columns, "rec", [(r, r ^ 1) for r in range(recs)])
    edge = edge_after(column_sums, guess[0], emission[0], logs)
    before = lax.ppermute(edge, "tm", [(t, t + 1) for t in range(size - 1)])
    combined = product_call(odd_kernel, "odd_product", LIGHT, [tile, lower, row_sums, before])
    forward, frame_logscale = sweeps(before, guess[0], emission[0], start, columns, others, combined)
    level = mean_after(all_logs, frame_logscale)[0, :1]
    told = lax.ppermute(level, "tm", over)
    sums_got = lax.ppermute(row_sums_again, "tm", back)
    combined = product_call(
        even_kernel, "even_product", LIGHT, [tile, got, column_sums, sums_got], combined, (frame_logscale,)
    )
    return combined[None], jnp.where(even, level, told), forward[None], frame_logscale


def solution(mesh):
    return jax.shard_map(
        local,
        mesh=mesh,
        in_specs=(
            P("rec", "tm", None, None),
            P("rec", "tm", None),
            P("rec", "tm", None),
            P(None, "rec"),
            P("rec", None),
        ),
        out_specs=(P("rec", "tm", None), P("rec"), P("rec", "tm", None), P("rec", "tm")),
        check_vma=False,
    )
```

time: 239 us -> 76.4 us (0.32)
  the two profiles are of different devices: /device:TPU:16 before, /device:TPU:8 now
where the time goes in v1:
time: 76.4 us; the launch traced here: 75.7 us
  starting transfers between devices  37.6 us (49%)
  waiting for transfers between devices  16 us (21%)
  Pallas kernels  12.6 us (16%)
  local copies, waits for them, and re-layouts  6.1 us (8%)
  between operations  2.68 us (4%)
    all_to_all x1, starting transfers between devices, local(): lax.all_to_all(logs, ('rec', 'tm'), 0, 0, tiled=True, axis_index_groups=p...  9.87 us
    all_to_all x1, starting transfers between devices, local(): lax.all_to_all(copies, 'rec', 0, 0, tiled=True, axis_index_groups=cores)  9.3 us
    ppermute x1, waiting for transfers between devices, local(): lax.ppermute(column_sums, 'tm', [(t, (t + 2) % size) for t in range(0, si...  8 us
    ppermute x1, starting transfers between devices, local(): told = lax.ppermute(level, 'tm', over)  7.03 us
    pallas_call x1, Pallas kernels, sweeps(): pl.pallas_call(sweep_kernel, in_specs=[pl.BlockSpec(memory_space=VMEM)] *...  5.88 us
    pallas_call x2, Pallas kernels, product_call(): pl.pallas_call(kernel, in_specs=specs + [pl.BlockSpec(memory_space=pl.ANY...  4.97 us
    ppermute x1, waiting for transfers between devices, local(): before = lax.ppermute(edge, 'tm', [(t, t + 1) for t in range(size - 1)])  4.75 us
    unnamed x16, local copies, waits for them, and re-layouts  4 us
  transfers between devices with their start and end apart: 10, of which 4 were waited for; matrix products, arithmetic and copies ran while one was open for 4% of the time, Pallas kernels for 12%

profile of v1, /device:TPU:8, one launch (start us, length us, event | category | flops | bytes accessed | tf_op | source)
XLA Modules:
  0.0 75.7 jit_solution(9913281937059342863)
XLA Ops:
  0.6 1.4 %collective-permute-start = (bf16[1024,1024]{1,0:T(8,128)(2,1)}, bf16[1024,1024]{1,0:T(8,128)(2,1)}, u32[]{:S(2)}, u32[]{:S(2)}) collective-permute-start(bf16[1024,1024]{1,0:T(8,128)(2,1)} %bitcast.16), channel_id=1, source_target_pairs={{1,0},{3,2},{5,4},{7,6},{9,8},{11,10},{13,12},{15,14},{17,16},{19,... | collective-permute-start | bytes 6291464 | tf_op jit(solution)/shard_map/ppermute | solution.py:229
  2.1 2.1 %broadcast_in_dim.20 = bf16[4,1024,128]{2,1,0:T(8,128)(2,1)} broadcast(bf16[1024,128]{1,0:T(8,128)(2,1)} %param.8), dimensions={1,2} | broadcast | bytes 1310720 | tf_op jit(solution)/shard_map/broadcast_in_dim | solution.py:230
  4.2 9.3 %all-to-all-start = ((bf16[4,1024,128]{2,1,0:T(8,128)(2,1)}), bf16[4,1024,128]{2,1,0:T(8,128)(2,1)S(1)}, u32[]{:S(2)}, u32[]{:S(2)}) async-start(bf16[4,1024,128]{2,1,0:T(8,128)(2,1)} %broadcast_in_dim.20), calls=%async_computation | async-start | bytes 2097152 | tf_op jit(solution)/shard_map/all_to_all | solution.py:231
  13.5 0.7 convert_reduce_fusion
  14.2 1.9 %collective-permute-start.1 = (f32[1,1024]{1,0:T(1,128)S(1)}, f32[1,1024]{1,0:T(1,128)S(1)}, u32[]{:S(2)}, u32[]{:S(2)}) collective-permute-start(f32[1,1024]{1,0:T(1,128)S(1)} %bitcast.29), channel_id=1, source_target_pairs={{0,2},{2,4},{4,6},{6,8},{8,10},{10,12},{12,14},{14,16},{16,18},{18... | collective-permute-start | bytes 12296 | tf_op jit(solution)/shard_map/ppermute | solution.py:234
  16.1 1.3 %collective-permute-start.2 = (f32[1,1024]{1,0:T(1,128)S(1)}, f32[1,1024]{1,0:T(1,128)S(1)}, u32[]{:S(2)}, u32[]{:S(2)}) collective-permute-start(f32[1,1024]{1,0:T(1,128)S(1)} %bitcast.26), channel_id=1, source_target_pairs={{1,2},{3,4},{5,6},{7,8},{9,10},{11,12},{13,14},{15,16},{17,18},{19... | collective-permute-start | bytes 12296 | tf_op jit(solution)/shard_map/ppermute | solution.py:235
  17.4 8.0 %collective-permute-done.1.column_sums = f32[1,1024]{1,0:T(1,128)S(1)} collective-permute-done((f32[1,1024]{1,0:T(1,128)S(1)}, f32[1,1024]{1,0:T(1,128)S(1)}, u32[]{:S(2)}, u32[]{:S(2)}) %collective-permute-start.1) | collective-permute-done | bytes 4128 | tf_op jit(solution)/shard_map/ppermute | solution.py:234
  25.4 2.6 %collective-permute-done.2.row_sums = f32[1,1024]{1,0:T(1,128)S(1)} collective-permute-done((f32[1,1024]{1,0:T(1,128)S(1)}, f32[1,1024]{1,0:T(1,128)S(1)}, u32[]{:S(2)}, u32[]{:S(2)}) %collective-permute-start.2) | collective-permute-done | bytes 4128 | tf_op jit(solution)/shard_map/ppermute | solution.py:235
  28.0 0.7 log_total.1
  28.7 1.0 %rows.1 = bf16[512,1024]{1,0:T(8,128)(2,1)} custom-call(bf16[1024,1024]{1,0:T(8,128)(2,1)S(1)} %bitcast.17, f32[32,128]{1,0:T(8,128)} %get-tuple-element.9.order), custom_call_target="tpu_custom_call" | custom-call | flops 1 | bytes 1 | tf_op jit(solution)/shard_map/rows/pallas_call | solution.py:76
  29.7 2.2 %collective-permute-start.4 = (bf16[512,1024]{1,0:T(8,128)(2,1)}, bf16[512,1024]{1,0:T(8,128)(2,1)}, u32[]{:S(2)}, u32[]{:S(2)}) collective-permute-start(bf16[512,1024]{1,0:T(8,128)(2,1)} %rows.1), channel_id=1, source_target_pairs={{0,1},{2,3},{4,5},{6,7},{8,9},{10,11},{12,13},{14,15},{16,17},{18,... | collective-permute-start | bytes 3145736 | tf_op jit(solution)/shard_map/ppermute | solution.py:237
  32.0 1.9 %collective-permute-start.6 = (bf16[4,1024,128]{2,1,0:T(8,128)(2,1)S(1)}, bf16[4,1024,128]{2,1,0:T(8,128)(2,1)}, u32[]{:S(2)}, u32[]{:S(2)}) collective-permute-start(bf16[4,1024,128]{2,1,0:T(8,128)(2,1)S(1)} %all-to-all-done.columns), channel_id=1, source_target_pairs={{0,64},{64,0},{128,192},{192,128},{256,320},{320,256},{384,448},{4... | collective-permute-start | bytes 3145736 | tf_op jit(solution)/shard_map/ppermute | solution.py:239
  33.9 9.9 %all-to-all-start.1 = ((f32[32,1,128]{2,1,0:T(1,128)}), f32[32,1,128]{2,1,0:T(1,128)S(1)}, u32[]{:S(2)}, u32[]{:S(2)}) async-start(f32[32,1,128]{2,1,0:T(1,128)} %bitcast.8), calls=%async_computation.1 | async-start | bytes 32768 | tf_op jit(solution)/shard_map/all_to_all | solution.py:238
  43.8 1.0 %copy-done.2 = bf16[1,256,1024]{2,1,0:T(8,128)(2,1)S(1)} copy-done((bf16[1,256,1024]{2,1,0:T(8,128)(2,1)S(1)}, bf16[1,256,1024]{2,1,0:T(8,128)(2,1)}, u32[]{:S(2)}) %copy-start.2) | copy-done | bytes 524312
  44.8 1.0 %copy-done.4 = bf16[1,256,1024]{2,1,0:T(8,128)(2,1)S(1)} copy-done((bf16[1,256,1024]{2,1,0:T(8,128)(2,1)S(1)}, bf16[1,256,1024]{2,1,0:T(8,128)(2,1)}, u32[]{:S(2)}) %copy-start.4) | copy-done | bytes 524312
  45.9 1.3 %collective-permute-start.5 = (f32[8,1024]{1,0:T(8,128)S(1)}, f32[8,1024]{1,0:T(8,128)S(1)}, u32[]{:S(2)}, u32[]{:S(2)}) collective-permute-start(f32[8,1024]{1,0:T(8,128)S(1)} %edge.1), channel_id=1, source_target_pairs={{0,1},{1,2},{2,3},{3,4},{4,5},{5,6},{6,7},{7,8},{8,9},{9,10},{10,1... | collective-permute-start | bytes 98312 | tf_op jit(solution)/shard_map/ppermute | solution.py:241
  47.2 1.3 %collective-permute-start.3 = (f32[1,1024]{1,0:T(1,128)S(1)}, f32[1,1024]{1,0:T(1,128)S(1)}, u32[]{:S(2)}, u32[]{:S(2)}) collective-permute-start(f32[1,1024]{1,0:T(1,128)S(1)} %get-tuple-element.8), channel_id=1, source_target_pairs={{1,0},{3,2},{5,4},{7,6},{9,8},{11,10},{13,12},{15,14},{17,16},{19,... | collective-permute-start | bytes 12296 | tf_op jit(solution)/shard_map/ppermute | solution.py:246
  48.5 4.7 %collective-permute-done.5.before = f32[8,1024]{1,0:T(8,128)S(1)} collective-permute-done((f32[8,1024]{1,0:T(8,128)S(1)}, f32[8,1024]{1,0:T(8,128)S(1)}, u32[]{:S(2)}, u32[]{:S(2)}) %collective-permute-start.5) | collective-permute-done | bytes 32800 | tf_op jit(solution)/shard_map/ppermute | solution.py:241
  53.3 1.3 %odd_product.1.order.other = bf16[512,1024]{1,0:T(8,128)(2,1)} custom-call(bf16[1024,1024]{1,0:T(8,128)(2,1)S(1)} %bitcast.18, bf16[512,1024]{1,0:T(8,128)(2,1)} %collective-permute-done.4.lower, f32[1,1024]{1,0:T(1,128)S(1)} %bitcast.28, f32[8,1024]{1,0:T(8,128)S(1)} %collective-permute-done.5.before), custom_call_target="tpu_custom_call" | custom-call | flops 1 | bytes 1 | tf_op jit(solution)/shard_map/odd_product/pallas_call | solution.py:189
  54.6 1.2 %copy-done.1 = bf16[512,1024]{1,0:T(8,128)(2,1)S(1)} copy-done((bf16[512,1024]{1,0:T(8,128)(2,1)S(1)}, bf16[512,1024]{1,0:T(8,128)(2,1)}, u32[]{:S(2)}) %copy-start.1) | copy-done | bytes 1048600
  55.8 5.9 %sweeps.1 = (bf16[256,1024]{1,0:T(8,128)(2,1)}, f32[1,256]{1,0:T(1,128)}) custom-call(f32[8,1024]{1,0:T(8,128)S(1)} %collective-permute-done.5.before, bf16[256,1024]{1,0:T(8,128)(2,1)S(1)} %bitcast.22, bf16[256,1024]{1,0:T(8,128)(2,1)S(1)} %bitcast.24, bf16[1,1024]{1,0:T(2,128)(2,1)S(1)} %copy-done.6, bf16[4,1024,128]{2,1,0:T(8,128)(2,1)S(1)} %all-to-all-done.columns, ...), custom_call_target="tpu_custom_call" | custom-call | flops 1 | bytes 1 | tf_op jit(solution)/shard_map/sweeps/pallas_call | solution.py:140
  62.4 7.0 %collective-permute-start.7 = (f32[1]{0:T(128)S(1)}, f32[1]{0:T(128)}, u32[]{:S(2)}, u32[]{:S(2)}) collective-permute-start(f32[1]{0:T(128)S(1)} %bitcast.32), channel_id=1, source_target_pairs={{0,1},{2,3},{4,5},{6,7},{8,9},{10,11},{12,13},{14,15},{16,17},{18,... | collective-permute-start | bytes 20 | tf_op jit(solution)/shard_map/ppermute | solution.py:245
  69.4 0.7 collective-permute-done.7
  70.8 3.7 %even_product.1 = bf16[512,1024]{1,0:T(8,128)(2,1)} custom-call(bf16[1024,1024]{1,0:T(8,128)(2,1)S(1)} %bitcast.19, bf16[1024,1024]{1,0:T(8,128)(2,1)} %collective-permute-done.got, f32[1,1024]{1,0:T(1,128)S(1)} %bitcast.31, f32[1,1024]{1,0:T(1,128)S(1)} %collective-permute-done.3.sums_got, ...), custom_call_target="tpu_custom_call", output_to_operand_aliasing={{}: (4, {})} | custom-call | flops 1 | bytes 1 | tf_op jit(solution)/shard_map/even_product/pallas_call | solution.py:189
  (21 shorter events, 0.8 us)
Async XLA Ops:
  0.6 12.8 %copy-start = (bf16[1,1,1024,1024]{3,2,1,0:T(8,128)(2,1)S(1)}, bf16[1,1,1024,1024]{3,2,1,0:T(8,128)(2,1)}, u32[]{:S(2)}) copy-start(bf16[1,1,1024,1024]{3,2,1,0:T(8,128)(2,1)} %param.5) | copy-start | bytes 6291460
  0.6 70.2 %collective-permute-start = (bf16[1024,1024]{1,0:T(8,128)(2,1)}, bf16[1024,1024]{1,0:T(8,128)(2,1)}, u32[]{:S(2)}, u32[]{:S(2)}) collective-permute-start(bf16[1024,1024]{1,0:T(8,128)(2,1)} %bitcast.16), channel_id=1, source_target_pairs={{1,0},{3,2},{5,4},{7,6},{9,8},{11,10},{13,12},{15,14},{17,16},{19,... | collective-permute-start | bytes 6291464 | tf_op jit(solution)/shard_map/ppermute | solution.py:229
  4.2 27.8 %all-to-all-start = ((bf16[4,1024,128]{2,1,0:T(8,128)(2,1)}), bf16[4,1024,128]{2,1,0:T(8,128)(2,1)S(1)}, u32[]{:S(2)}, u32[]{:S(2)}) async-start(bf16[4,1024,128]{2,1,0:T(8,128)(2,1)} %broadcast_in_dim.20), calls=%async_computation | async-start | bytes 2097152 | tf_op jit(solution)/shard_map/all_to_all | solution.py:231
  14.2 11.2 %collective-permute-start.1 = (f32[1,1024]{1,0:T(1,128)S(1)}, f32[1,1024]{1,0:T(1,128)S(1)}, u32[]{:S(2)}, u32[]{:S(2)}) collective-permute-start(f32[1,1024]{1,0:T(1,128)S(1)} %bitcast.29), channel_id=1, source_target_pairs={{0,2},{2,4},{4,6},{6,8},{8,10},{10,12},{12,14},{14,16},{16,18},{18... | collective-permute-start | bytes 12296 | tf_op jit(solution)/shard_map/ppermute | solution.py:234
  16.1 11.9 %collective-permute-start.2 = (f32[1,1024]{1,0:T(1,128)S(1)}, f32[1,1024]{1,0:T(1,128)S(1)}, u32[]{:S(2)}, u32[]{:S(2)}) collective-permute-start(f32[1,1024]{1,0:T(1,128)S(1)} %bitcast.26), channel_id=1, source_target_pairs={{1,2},{3,4},{5,6},{7,8},{9,10},{11,12},{13,14},{15,16},{17,18},{19... | collective-permute-start | bytes 12296 | tf_op jit(solution)/shard_map/ppermute | solution.py:235
  29.7 23.5 %collective-permute-start.4 = (bf16[512,1024]{1,0:T(8,128)(2,1)}, bf16[512,1024]{1,0:T(8,128)(2,1)}, u32[]{:S(2)}, u32[]{:S(2)}) collective-permute-start(bf16[512,1024]{1,0:T(8,128)(2,1)} %rows.1), channel_id=1, source_target_pairs={{0,1},{2,3},{4,5},{6,7},{8,9},{10,11},{12,13},{14,15},{16,17},{18,... | collective-permute-start | bytes 3145736 | tf_op jit(solution)/shard_map/ppermute | solution.py:237
  32.0 22.6 %collective-permute-start.6 = (bf16[4,1024,128]{2,1,0:T(8,128)(2,1)S(1)}, bf16[4,1024,128]{2,1,0:T(8,128)(2,1)}, u32[]{:S(2)}, u32[]{:S(2)}) collective-permute-start(bf16[4,1024,128]{2,1,0:T(8,128)(2,1)S(1)} %all-to-all-done.columns), channel_id=1, source_target_pairs={{0,64},{64,0},{128,192},{192,128},{256,320},{320,256},{384,448},{4... | collective-permute-start | bytes 3145736 | tf_op jit(solution)/shard_map/ppermute | solution.py:239
  33.9 27.8 %all-to-all-start.1 = ((f32[32,1,128]{2,1,0:T(1,128)}), f32[32,1,128]{2,1,0:T(1,128)S(1)}, u32[]{:S(2)}, u32[]{:S(2)}) async-start(f32[32,1,128]{2,1,0:T(1,128)} %bitcast.8), calls=%async_computation.1 | async-start | bytes 32768 | tf_op jit(solution)/shard_map/all_to_all | solution.py:238
  43.8 1.0 %copy-start.2 = (bf16[1,256,1024]{2,1,0:T(8,128)(2,1)S(1)}, bf16[1,256,1024]{2,1,0:T(8,128)(2,1)}, u32[]{:S(2)}) copy-start(bf16[1,256,1024]{2,1,0:T(8,128)(2,1)} %param.6) | copy-start | bytes 1572868
  44.8 1.0 %copy-start.4 = (bf16[1,256,1024]{2,1,0:T(8,128)(2,1)S(1)}, bf16[1,256,1024]{2,1,0:T(8,128)(2,1)}, u32[]{:S(2)}) copy-start(bf16[1,256,1024]{2,1,0:T(8,128)(2,1)} %param.7) | copy-start | bytes 1572868
  45.9 7.4 %collective-permute-start.5 = (f32[8,1024]{1,0:T(8,128)S(1)}, f32[8,1024]{1,0:T(8,128)S(1)}, u32[]{:S(2)}, u32[]{:S(2)}) collective-permute-start(f32[8,1024]{1,0:T(8,128)S(1)} %edge.1), channel_id=1, source_target_pairs={{0,1},{1,2},{2,3},{3,4},{4,5},{5,6},{6,7},{7,8},{8,9},{9,10},{10,1... | collective-permute-start | bytes 98312 | tf_op jit(solution)/shard_map/ppermute | solution.py:241
  47.2 23.7 %collective-permute-start.3 = (f32[1,1024]{1,0:T(1,128)S(1)}, f32[1,1024]{1,0:T(1,128)S(1)}, u32[]{:S(2)}, u32[]{:S(2)}) collective-permute-start(f32[1,1024]{1,0:T(1,128)S(1)} %get-tuple-element.8), channel_id=1, source_target_pairs={{1,0},{3,2},{5,4},{7,6},{9,8},{11,10},{13,12},{15,14},{17,16},{19,... | collective-permute-start | bytes 12296 | tf_op jit(solution)/shard_map/ppermute | solution.py:246
  48.5 6.1 %copy-start.3 = (bf16[1,256,1024]{2,1,0:T(8,128)(2,1)S(1)}, bf16[1,256,1024]{2,1,0:T(8,128)(2,1)}, u32[]{:S(2)}) copy-start(bf16[1,256,1024]{2,1,0:T(8,128)(2,1)} %param.6) | copy-start | bytes 1572868
  48.5 6.1 %copy-start.5 = (bf16[1,256,1024]{2,1,0:T(8,128)(2,1)S(1)}, bf16[1,256,1024]{2,1,0:T(8,128)(2,1)}, u32[]{:S(2)}) copy-start(bf16[1,256,1024]{2,1,0:T(8,128)(2,1)} %param.7) | copy-start | bytes 1572868
  48.5 6.1 %copy-start.6 = (bf16[1,1024]{1,0:T(2,128)(2,1)S(1)}, bf16[1,1024]{1,0:T(2,128)(2,1)}, u32[]{:S(2)}) copy-start(bf16[1,1024]{1,0:T(2,128)(2,1)} %start.1) | copy-start | bytes 6148
  54.6 1.2 %copy-start.1 = (bf16[512,1024]{1,0:T(8,128)(2,1)S(1)}, bf16[512,1024]{1,0:T(8,128)(2,1)}, u32[]{:S(2)}) copy-start(bf16[512,1024]{1,0:T(8,128)(2,1)} %odd_product.1.order.other) | copy-start | bytes 3145732
  61.7 0.7 copy-start.7
  62.4 7.7 %collective-permute-start.7 = (f32[1]{0:T(128)S(1)}, f32[1]{0:T(128)}, u32[]{:S(2)}, u32[]{:S(2)}) collective-permute-start(f32[1]{0:T(128)S(1)} %bitcast.32), channel_id=1, source_target_pairs={{0,1},{2,3},{4,5},{6,7},{8,9},{10,11},{12,13},{14,15},{16,17},{18,... | collective-permute-start | bytes 20 | tf_op jit(solution)/shard_map/ppermute | solution.py:245

commit v2 on v1

v2 whole, which is shorter than its diff:
```python
import functools

import jax
import jax.numpy as jnp
from jax import lax
from jax.experimental import pallas as pl
from jax.experimental.pallas import tpu as pltpu
from jax.sharding import PartitionSpec as P

SWEEPS = 4
EDGE = 16
F32 = jnp.float32
BF16 = jnp.bfloat16
VMEM = pltpu.VMEM
HBM = pltpu.HBM
TOTAL_COST = pl.CostEstimate(flops=12 * 10**9, bytes_accessed=24 * 10**6, transcendentals=0)
LIGHT = pl.CostEstimate(flops=1, bytes_accessed=1, transcendentals=0)


def parity():
    return lax.rem(lax.axis_index("tm"), 2)


def params(mib=24):
    return pltpu.CompilerParams(vmem_limit_bytes=mib * 1024 * 1024)


def matmul(a, b):
    return jnp.dot(a, b, preferred_element_type=F32)


def edge_kernel(column_sums, row_sums, guess, emit, out):
    row = lax.broadcasted_iota(jnp.int32, out.shape, 0)
    sums = jnp.where(parity() == 0, column_sums[...], row_sums[...])
    rows = pltpu.roll(guess[...].astype(F32)[8:], 5, 0)
    out[...] = jnp.where(row == 0, sums, jnp.where(row < 5, rows, emit[...].astype(F32)[8:]))


def make_edge(column_sums, row_sums, guess_rows, emit_rows):
    states = guess_rows.shape[1]
    last = guess_rows.shape[0] // EDGE - 1
    tail = pl.BlockSpec((EDGE, states), lambda i: (last, 0))
    return pl.pallas_call(
        edge_kernel,
        grid=(1,),
        in_specs=[pl.BlockSpec((1, states), lambda i: (0, 0))] * 2 + [tail, tail],
        out_specs=pl.BlockSpec((8, states), lambda i: (0, 0)),
        out_shape=jax.ShapeDtypeStruct((8, states), F32),
        compiler_params=params(),
        cost_estimate=LIGHT,
        name="edge",
    )(column_sums, row_sums, guess_rows, emit_rows)


def total_kernel(column_sums, before, order, totals):
    value = jnp.sum(column_sums[...] * before[0:1], axis=1, keepdims=True)
    totals[...] = jnp.broadcast_to(value, totals.shape)


def pair_total(column_sums, before, peers, order):
    return pl.pallas_call(
        total_kernel,
        in_specs=[pl.BlockSpec(memory_space=VMEM)] * 2 + [pl.BlockSpec(memory_space=pl.ANY)],
        out_shape=jax.ShapeDtypeStruct((peers, 128), F32),
        compiler_params=params(),
        cost_estimate=TOTAL_COST,
        name="pair_total",
    )(column_sums, before, order)


def copies_kernel(shard, out):
    for c in range(out.shape[0]):
        out[c] = shard[...]


def copies_of(shard, count):
    return pl.pallas_call(
        copies_kernel,
        out_shape=jax.ShapeDtypeStruct((count,) + shard.shape, BF16),
        compiler_params=params(),
        cost_estimate=LIGHT,
        name="copies",
    )(shard)


def sweep_kernel(
    before, start, guess_in, emit_in, columns, others, out, logscale, token, guess, emit, held, table, row_sems, sems
):
    blocks, states, width = columns.shape
    frames = guess.shape[0]
    first = lax.axis_index("tm") == 0
    core = lax.rem(lax.axis_index("rec"), 2)

    def table_loads(mine):
        copies = []
        for b in range(blocks):
            for k, ref in enumerate((columns, others)):
                at = (2 * b + (mine if k == 0 else 1 - mine)) * width
                copies.append(pltpu.make_async_copy(ref.at[b], table.at[:, pl.ds(at, width)], sems.at[2 * b + k]))
        return copies

    row_loads = [
        pltpu.make_async_copy(guess_in, guess, row_sems.at[0]),
        pltpu.make_async_copy(emit_in, emit, row_sems.at[1]),
    ]
    for copy in row_loads:
        copy.start()
    for mine in range(2):

        @pl.when(core == mine)
        def _():
            for copy in table_loads(mine):
                copy.start()

    for copy in row_loads:
        copy.wait()
    edge = before[...]
    blank = jnp.zeros_like(edge)
    rows = frames + EDGE
    lead = SWEEPS
    prior = jnp.concatenate([blank, pltpu.roll(edge, 3, 0), guess[...].astype(F32)], axis=0)
    prior = pltpu.roll(prior, rows - (EDGE - lead), 0)
    emission = jnp.concatenate([blank, edge, emit[...].astype(F32)], axis=0)
    row = lax.broadcasted_iota(jnp.int32, (rows, 1), 0)
    start_row = start[...].astype(F32)
    held[...] = jnp.where(jnp.logical_and(first, row == lead - 1), start_row, prior).astype(BF16)
    for copy in table_loads(0):
        copy.wait()
    for m in range(1, SWEEPS + 1):
        now = rows if m < SWEEPS else frames
        shifted = pltpu.roll(emission, rows - (EDGE - lead + m), 0)[:now]
        unscaled = []
        for b in range(blocks):
            where = slice(2 * b * width, 2 * (b + 1) * width)
            unscaled.append(matmul(held[:now, :], table[:, where]) * shifted[:, where])
        lanes = sum(u[:, :128] + u[:, 128:] for u in unscaled)
        mean = jnp.sum(lanes, axis=1, keepdims=True) * (1.0 / states)
        inverse = 1.0 / mean
        for b, u in enumerate(unscaled):
            where = slice(2 * b * width, 2 * (b + 1) * width)
            scaled = u * inverse
            if m < SWEEPS:
                fixed = jnp.logical_and(first, row == lead - 1 - m)
                held[:, where] = jnp.where(fixed, start_row[:, where], scaled).astype(BF16)
            else:
                out[:, where] = scaled.astype(BF16)
        if m == SWEEPS:
            logscale[...] = jnp.transpose(jnp.broadcast_to(jnp.log(mean), (frames, 128)))[0:1, :]
    token[...] = jnp.zeros_like(token)


def sweeps(before, guess, emit, start, columns, others):
    frames, states = guess.shape
    return pl.pallas_call(
        sweep_kernel,
        in_specs=[pl.BlockSpec(memory_space=VMEM)] * 2 + [pl.BlockSpec(memory_space=pl.ANY)] * 4,
        out_shape=(
            jax.ShapeDtypeStruct((frames, states), BF16),
            jax.ShapeDtypeStruct((1, frames), F32),
            jax.ShapeDtypeStruct((8, 128), F32),
        ),
        scratch_shapes=[
            VMEM((frames, states), BF16),
            VMEM((frames, states), BF16),
            VMEM((frames + EDGE, states), BF16),
            VMEM((states, states), BF16),
            pltpu.SemaphoreType.DMA((2,)),
            pltpu.SemaphoreType.DMA((2 * columns.shape[0],)),
        ],
        compiler_params=params(),
        cost_estimate=LIGHT,
        name="sweeps",
    )(before, start, guess, emit, columns, others)


def product_kernel(
    own, lower, got, column_sums, sums_got, row_sums, before, order, out, token, right, total, result, load_sems, out_sems
):
    states = own.shape[0]
    parts, depth, _ = right.shape
    half = states // 2
    even = parity() == 0
    token[...] = jnp.zeros_like(token)

    def store(p):
        rows = pl.ds(p * (half // parts), half // parts)
        return pltpu.make_async_copy(result.at[rows, :], out.at[rows, :], out_sems.at[p])

    def finish(scale):
        for p in range(parts):
            rows = slice(p * (half // parts), (p + 1) * (half // parts))
            result[rows, :] = (total[rows, :] * scale).astype(BF16)
            store(p).start()

    @pl.when(even)
    def _():
        loads = [
            pltpu.make_async_copy(got.at[pl.ds(p * depth, depth), :], right.at[p], load_sems.at[p]) for p in range(parts)
        ]
        for load in loads:
            load.start()
        scale = (states * states) / jnp.sum(column_sums[...] * sums_got[...], axis=1, keepdims=True)
        for p in range(parts):
            loads[p].wait()
            block = matmul(own[:half, p * depth : (p + 1) * depth], right[p])
            total[...] = block if p == 0 else total[...] + block
        finish(scale)

    @pl.when(jnp.logical_not(even))
    def _():
        scale = (states * states) / jnp.sum(row_sums[...] * before[0:1], axis=1, keepdims=True)
        total[...] = matmul(lower[...], own[...])
        finish(scale)

    for p in range(parts):
        store(p).wait()


def pair_product(own, lower, got, column_sums, sums_got, row_sums, before, order):
    states = own.shape[0]
    half, parts = states // 2, 4
    spaces = (VMEM, VMEM, pl.ANY, VMEM, VMEM, VMEM, VMEM, pl.ANY)
    return pl.pallas_call(
        product_kernel,
        in_specs=[pl.BlockSpec(memory_space=space) for space in spaces],
        out_specs=[pl.BlockSpec(memory_space=HBM), pl.BlockSpec(memory_space=VMEM)],
        out_shape=(jax.ShapeDtypeStruct((half, states), BF16), jax.ShapeDtypeStruct((8, 128), F32)),
        scratch_shapes=[
            VMEM((parts, states // parts, states), BF16),
            VMEM((half, states), F32),
            VMEM((half, states), BF16),
            pltpu.SemaphoreType.DMA((parts,)),
            pltpu.SemaphoreType.DMA((parts,)),
        ],
        compiler_params=params(),
        cost_estimate=LIGHT,
        name="pair_product",
    )(own, lower, got, column_sums, sums_got, row_sums, before, order)


def mean_kernel(states, totals, order, level):
    logs = jnp.log(totals[...] * (1.0 / states))
    level[...] = jnp.sum(logs, axis=0, keepdims=True) * (1.0 / logs.shape[0])


def mean_log(totals, states, order):
    return pl.pallas_call(
        functools.partial(mean_kernel, states),
        in_specs=[pl.BlockSpec(memory_space=VMEM), pl.BlockSpec(memory_space=pl.ANY)],
        out_shape=jax.ShapeDtypeStruct((1, 128), F32),
        compiler_params=params(),
        cost_estimate=LIGHT,
        name="mean_log",
    )(totals, order)


def local(summary, guess, emission, transition, start):
    tile = summary[0, 0]
    states = tile.shape[0]
    size, recs = lax.axis_size("tm"), lax.axis_size("rec")
    even = lax.axis_index("tm") % 2 == 0
    back = [(t, t - 1) for t in range(1, size, 2)]
    over = [(t, t + 1) for t in range(0, size, 2)]
    planes = size // 4
    peers = [[r * size + t for t in range(0, size, 2)] for r in range(recs)]
    peers += [[r * size + t for r in range(recs) for t in range(z, size, planes)] for z in range(1, planes, 2)]
    cores = [list(range(c, recs, 2)) for c in range(2)]

    got = lax.ppermute(tile, "tm", back)
    copies = copies_of(transition, recs // 2)
    columns = lax.all_to_all(copies, "rec", 0, 0, tiled=True, axis_index_groups=cores)
    wide = tile.astype(F32)
    column_sums, row_sums = jnp.sum(wide, axis=0)[None], jnp.sum(wide, axis=1)[None]
    pair_columns = lax.ppermute(column_sums, "tm", [(t, (t + 2) % size) for t in range(0, size, 2)])
    edge = make_edge(column_sums, row_sums, guess[0], emission[0])
    before = lax.ppermute(edge, "tm", [(t, (t + 1) % size) for t in range(size)])
    lower = lax.ppermute(tile[states // 2 :], "tm", over)
    totals = pair_total(pair_columns, before, size // 2, lower)
    totals = lax.all_to_all(totals, ("rec", "tm"), 0, 0, tiled=True, axis_index_groups=peers)
    others = lax.ppermute(columns, "rec", [(r, r ^ 1) for r in range(recs)])
    sums_got = lax.ppermute(row_sums, "tm", back)
    forward, frame_logscale, token = sweeps(before, guess[0], emission[0], start, columns, others)
    combined, token = pair_product(tile, lower, got, column_sums, sums_got, row_sums, before, token)
    level = mean_log(totals, states, token)[0, :1]
    told = lax.ppermute(level, "tm", over)
    return combined[None], jnp.where(even, level, told), forward[None], frame_logscale


def solution(mesh):
    return jax.shard_map(
        local,
        mesh=mesh,
        in_specs=(
            P("rec", "tm", None, None),
            P("rec", "tm", None),
            P("rec", "tm", None),
            P(None, "rec"),
            P("rec", None),
        ),
        out_specs=(P("rec", "tm", None), P("rec"), P("rec", "tm", None), P("rec", "tm")),
        check_vma=False,
    )
```

time: 76.4 us -> 71.3 us (0.933)
  the two profiles are of different devices: /device:TPU:8 before, /device:TPU:34 now
where the time goes in v2:
time: 71.3 us; the launch traced here: 70.6 us
  starting transfers between devices  35.9 us (50%)
  waiting for transfers between devices  14.8 us (21%)
  Pallas kernels  10.6 us (15%)
  local copies, waits for them, and re-layouts  5.93 us (8%)
  between operations  2.61 us (4%)
  other arithmetic  0.72 us (1%)
    ppermute x1, starting transfers between devices, local(): sums_got = lax.ppermute(row_sums, 'tm', back)  11.9 us
    all_to_all x1, waiting for transfers between devices, local(): lax.all_to_all(copies, 'rec', 0, 0, tiled=True, axis_index_groups=cores)  10.7 us
    ppermute x1, starting transfers between devices, local(): got = lax.ppermute(tile, 'tm', back)  6.84 us
    all_to_all x1, starting transfers between devices, local(): lax.all_to_all(totals, ('rec', 'tm'), 0, 0, tiled=True, axis_index_groups...  5.7 us
    pallas_call x1, Pallas kernels, sweeps(): pl.pallas_call(sweep_kernel, in_specs=[pl.BlockSpec(memory_space=VMEM)] *...  5.37 us
    all_to_all x1, starting transfers between devices, local(): lax.all_to_all(copies, 'rec', 0, 0, tiled=True, axis_index_groups=cores)  4.46 us
    ppermute x1, waiting for transfers between devices, local(): told = lax.ppermute(level, 'tm', over)  4.09 us
    unnamed x14, local copies, waits for them, and re-layouts  3.52 us
  transfers between devices with their start and end apart: 9, of which 2 were waited for; matrix products, arithmetic and copies ran while one was open for 1% of the time, Pallas kernels for 15%

profile of v2, /device:TPU:34, one launch (start us, length us, event | category | flops | bytes accessed | tf_op | source)
XLA Modules:
  0.0 70.6 jit_solution(10589502480207524134)
XLA Ops:
  0.6 2.4 %slice_bitcast_fusion = bf16[512,1024]{1,0:T(8,128)(2,1)} fusion(bf16[1,1,1024,1024]{3,2,1,0:T(8,128)(2,1)} %param.5), kind=kLoop, calls=%fused_computation.2 | loop fusion | bytes 2097152 | tf_op jit(solution)/shard_map/slice | solution.py:277
  3.1 1.3 %collective-permute-start = (bf16[512,1024]{1,0:T(8,128)(2,1)}, bf16[512,1024]{1,0:T(8,128)(2,1)}, u32[]{:S(2)}, u32[]{:S(2)}) collective-permute-start(bf16[512,1024]{1,0:T(8,128)(2,1)} %slice_bitcast_fusion), channel_id=1, source_target_pairs={{0,1},{2,3},{4,5},{6,7},{8,9},{10,11},{12,13},{14,15},{16,17},{18,... | collective-permute-start | bytes 3145736 | tf_op jit(solution)/shard_map/ppermute | solution.py:277
  4.3 6.8 %collective-permute-start.1 = (bf16[1024,1024]{1,0:T(8,128)(2,1)S(1)}, bf16[1024,1024]{1,0:T(8,128)(2,1)}, u32[]{:S(2)}, u32[]{:S(2)}) collective-permute-start(bf16[1024,1024]{1,0:T(8,128)(2,1)S(1)} %bitcast.18), channel_id=1, source_target_pairs={{1,0},{3,2},{5,4},{7,6},{9,8},{11,10},{13,12},{15,14},{17,16},{19,... | collective-permute-start | bytes 6291464 | tf_op jit(solution)/shard_map/ppermute | solution.py:269
  11.2 0.9 %copy-done.5 = bf16[1024,128]{1,0:T(8,128)(2,1)S(1)} copy-done((bf16[1024,128]{1,0:T(8,128)(2,1)S(1)}, bf16[1024,128]{1,0:T(8,128)(2,1)}, u32[]{:S(2)}) %copy-start.5) | copy-done | bytes 262168
  12.1 1.1 %copies.1 = bf16[4,1024,128]{2,1,0:T(8,128)(2,1)} custom-call(bf16[1024,128]{1,0:T(8,128)(2,1)S(1)} %copy-done.5), custom_call_target="tpu_custom_call" | custom-call | flops 1 | bytes 1 | tf_op jit(solution)/shard_map/copies/pallas_call | solution.py:77
  13.3 4.5 %all-to-all-start = ((bf16[4,1024,128]{2,1,0:T(8,128)(2,1)}), bf16[4,1024,128]{2,1,0:T(8,128)(2,1)S(1)}, u32[]{:S(2)}, u32[]{:S(2)}) async-start(bf16[4,1024,128]{2,1,0:T(8,128)(2,1)} %copies.1), calls=%async_computation | async-start | bytes 2097152 | tf_op jit(solution)/shard_map/all_to_all | solution.py:271
  17.7 0.7 %convert_reduce_fusion = (f32[1024]{0:T(1024)S(1)}, f32[1024]{0:T(1024)S(1)}) fusion(bf16[1,1,1024,1024]{3,2,1,0:T(8,128)(2,1)S(1)} %copy-done), kind=kLoop, calls=%fused_computation | loop fusion | flops 3143680 | bytes 2105344 | tf_op jit(solution)/shard_map/reduce_sum | solution.py:273
  18.4 0.3 copy-done.1
  18.8 0.2 copy-done.3
  18.9 0.0 copy-start.6
  18.9 1.9 %collective-permute-start.3 = (f32[8,1024]{1,0:T(8,128)S(1)}, f32[8,1024]{1,0:T(8,128)S(1)}, u32[]{:S(2)}, u32[]{:S(2)}) collective-permute-start(f32[8,1024]{1,0:T(8,128)S(1)} %edge.1), channel_id=1, source_target_pairs={{0,1},{1,2},{2,3},{3,4},{4,5},{5,6},{6,7},{7,8},{8,9},{9,10},{10,1... | collective-permute-start | bytes 98312 | tf_op jit(solution)/shard_map/ppermute | solution.py:276
  20.9 0.7 collective-permute-start.5
  21.5 10.7 %all-to-all-done.columns = bf16[4,1024,128]{2,1,0:T(8,128)(2,1)S(1)} async-done(((bf16[4,1024,128]{2,1,0:T(8,128)(2,1)}), bf16[4,1024,128]{2,1,0:T(8,128)(2,1)S(1)}, u32[]{:S(2)}, u32[]{:S(2)}) %all-to-all-start) | async-done | bytes 1048608 | tf_op jit(solution)/shard_map/all_to_all | solution.py:271
  32.3 1.9 %collective-permute-start.4 = (bf16[4,1024,128]{2,1,0:T(8,128)(2,1)S(1)}, bf16[4,1024,128]{2,1,0:T(8,128)(2,1)}, u32[]{:S(2)}, u32[]{:S(2)}) collective-permute-start(bf16[4,1024,128]{2,1,0:T(8,128)(2,1)S(1)} %all-to-all-done.columns), channel_id=1, source_target_pairs={{0,64},{64,0},{128,192},{192,128},{256,320},{320,256},{384,448},{4... | collective-permute-start | bytes 3145736 | tf_op jit(solution)/shard_map/ppermute | solution.py:280
  34.2 0.7 pair_total.1
  34.9 5.7 %all-to-all-start.1 = ((f32[32,1,128]{2,1,0:T(1,128)}), f32[32,1,128]{2,1,0:T(1,128)S(1)}, u32[]{:S(2)}, u32[]{:S(2)}) async-start(f32[32,1,128]{2,1,0:T(1,128)} %bitcast.9), calls=%async_computation.1 | async-start | bytes 32768 | tf_op jit(solution)/shard_map/all_to_all | solution.py:279
  40.6 11.9 %collective-permute-start.2 = (f32[1,1024]{1,0:T(1,128)S(1)}, f32[1,1024]{1,0:T(1,128)S(1)}, u32[]{:S(2)}, u32[]{:S(2)}) collective-permute-start(f32[1,1024]{1,0:T(1,128)S(1)} %bitcast.26), channel_id=1, source_target_pairs={{1,0},{3,2},{5,4},{7,6},{9,8},{11,10},{13,12},{15,14},{17,16},{19,... | collective-permute-start | bytes 12296 | tf_op jit(solution)/shard_map/ppermute | solution.py:281
  52.5 0.0 copy-start.2
  52.5 1.0 %copy-done.2 = bf16[1,256,1024]{2,1,0:T(8,128)(2,1)S(1)} copy-done((bf16[1,256,1024]{2,1,0:T(8,128)(2,1)S(1)}, bf16[1,256,1024]{2,1,0:T(8,128)(2,1)}, u32[]{:S(2)}) %copy-start.2) | copy-done | bytes 524312
  53.6 1.0 %copy-done.4 = bf16[1,256,1024]{2,1,0:T(8,128)(2,1)S(1)} copy-done((bf16[1,256,1024]{2,1,0:T(8,128)(2,1)S(1)}, bf16[1,256,1024]{2,1,0:T(8,128)(2,1)}, u32[]{:S(2)}) %copy-start.4) | copy-done | bytes 524312
  54.6 5.4 %sweeps.1 = (bf16[256,1024]{1,0:T(8,128)(2,1)}, f32[1,256]{1,0:T(1,128)}, f32[8,128]{1,0:T(8,128)S(1)}) custom-call(f32[8,1024]{1,0:T(8,128)S(1)} %collective-permute-done.3.before, bf16[1,1024]{1,0:T(2,128)(2,1)S(1)} %copy-done.6, bf16[256,1024]{1,0:T(8,128)(2,1)S(1)} %bitcast.21, bf16[256,1024]{1,0:T(8,128)(2,1)S(1)} %bitcast.23, ...), custom_call_target="tpu_custom_call" | custom-call | flops 1 | bytes 1 | tf_op jit(solution)/shard_map/sweeps/pallas_call | solution.py:154
  60.0 3.4 %pair_product.1 = (bf16[512,1024]{1,0:T(8,128)(2,1)}, f32[8,128]{1,0:T(8,128)S(1)}) custom-call(bf16[1024,1024]{1,0:T(8,128)(2,1)S(1)} %bitcast.19, bf16[512,1024]{1,0:T(8,128)(2,1)} %collective-permute-done.lower.order, bf16[1024,1024]{1,0:T(8,128)(2,1)} %collective-permute-done.1.got, f32[1,1024]{1,0:T(1,128)S(1)} %bitcast.30, ...), custom_call_target="tpu_custom_call" | custom-call | flops 1 | bytes 1 | tf_op jit(solution)/shard_map/pair_product/pallas_call | solution.py:223
  63.5 1.3 %collective-permute-start.6 = (f32[1]{0:T(128)S(1)}, f32[1]{0:T(128)}, u32[]{:S(2)}, u32[]{:S(2)}) collective-permute-start(f32[1]{0:T(128)S(1)} %bitcast.31), channel_id=1, source_target_pairs={{0,1},{2,3},{4,5},{6,7},{8,9},{10,11},{12,13},{14,15},{16,17},{18,... | collective-permute-start | bytes 20 | tf_op jit(solution)/shard_map/ppermute | solution.py:285
  64.8 4.1 %collective-permute-done.6 = f32[1]{0:T(128)} collective-permute-done((f32[1]{0:T(128)S(1)}, f32[1]{0:T(128)}, u32[]{:S(2)}, u32[]{:S(2)}) %collective-permute-start.6) | collective-permute-done | bytes 36 | tf_op jit(solution)/shard_map/ppermute | solution.py:285
  (16 shorter events, 0.1 us)
Async XLA Ops:
  0.6 3.7 %copy-start = (bf16[1,1,1024,1024]{3,2,1,0:T(8,128)(2,1)S(1)}, bf16[1,1,1024,1024]{3,2,1,0:T(8,128)(2,1)}, u32[]{:S(2)}) copy-start(bf16[1,1,1024,1024]{3,2,1,0:T(8,128)(2,1)} %param.5) | copy-start | bytes 6291460
  3.1 31.1 %collective-permute-start = (bf16[512,1024]{1,0:T(8,128)(2,1)}, bf16[512,1024]{1,0:T(8,128)(2,1)}, u32[]{:S(2)}, u32[]{:S(2)}) collective-permute-start(bf16[512,1024]{1,0:T(8,128)(2,1)} %slice_bitcast_fusion), channel_id=1, source_target_pairs={{0,1},{2,3},{4,5},{6,7},{8,9},{10,11},{12,13},{14,15},{16,17},{18,... | collective-permute-start | bytes 3145736 | tf_op jit(solution)/shard_map/ppermute | solution.py:277
  4.3 55.7 %collective-permute-start.1 = (bf16[1024,1024]{1,0:T(8,128)(2,1)S(1)}, bf16[1024,1024]{1,0:T(8,128)(2,1)}, u32[]{:S(2)}, u32[]{:S(2)}) collective-permute-start(bf16[1024,1024]{1,0:T(8,128)(2,1)S(1)} %bitcast.18), channel_id=1, source_target_pairs={{1,0},{3,2},{5,4},{7,6},{9,8},{11,10},{13,12},{15,14},{17,16},{19,... | collective-permute-start | bytes 6291464 | tf_op jit(solution)/shard_map/ppermute | solution.py:269
  11.2 0.9 %copy-start.5 = (bf16[1024,128]{1,0:T(8,128)(2,1)S(1)}, bf16[1024,128]{1,0:T(8,128)(2,1)}, u32[]{:S(2)}) copy-start(bf16[1024,128]{1,0:T(8,128)(2,1)} %shard.1) | copy-start | bytes 786436
  13.3 19.0 %all-to-all-start = ((bf16[4,1024,128]{2,1,0:T(8,128)(2,1)}), bf16[4,1024,128]{2,1,0:T(8,128)(2,1)S(1)}, u32[]{:S(2)}, u32[]{:S(2)}) async-start(bf16[4,1024,128]{2,1,0:T(8,128)(2,1)} %copies.1), calls=%async_computation | async-start | bytes 2097152 | tf_op jit(solution)/shard_map/all_to_all | solution.py:271
  17.7 1.0 %copy-start.1 = (bf16[1,256,1024]{2,1,0:T(8,128)(2,1)S(1)}, bf16[1,256,1024]{2,1,0:T(8,128)(2,1)}, u32[]{:S(2)}) copy-start(bf16[1,256,1024]{2,1,0:T(8,128)(2,1)} %param.6) | copy-start | bytes 1572868
  17.7 1.2 %copy-start.3 = (bf16[1,256,1024]{2,1,0:T(8,128)(2,1)S(1)}, bf16[1,256,1024]{2,1,0:T(8,128)(2,1)}, u32[]{:S(2)}) copy-start(bf16[1,256,1024]{2,1,0:T(8,128)(2,1)} %param.7) | copy-start | bytes 1572868
  18.9 33.6 %copy-start.6 = (bf16[1,1024]{1,0:T(2,128)(2,1)S(1)}, bf16[1,1024]{1,0:T(2,128)(2,1)}, u32[]{:S(2)}) copy-start(bf16[1,1024]{1,0:T(2,128)(2,1)} %start.1) | copy-start | bytes 6148
  18.9 15.2 %collective-permute-start.3 = (f32[8,1024]{1,0:T(8,128)S(1)}, f32[8,1024]{1,0:T(8,128)S(1)}, u32[]{:S(2)}, u32[]{:S(2)}) collective-permute-start(f32[8,1024]{1,0:T(8,128)S(1)} %edge.1), channel_id=1, source_target_pairs={{0,1},{1,2},{2,3},{3,4},{4,5},{5,6},{6,7},{7,8},{8,9},{9,10},{10,1... | collective-permute-start | bytes 98312 | tf_op jit(solution)/shard_map/ppermute | solution.py:276
  20.9 13.3 %collective-permute-start.5 = (f32[1,1024]{1,0:T(1,128)S(1)}, f32[1,1024]{1,0:T(1,128)S(1)}, u32[]{:S(2)}, u32[]{:S(2)}) collective-permute-start(f32[1,1024]{1,0:T(1,128)S(1)} %bitcast.29), channel_id=1, source_target_pairs={{0,2},{2,4},{4,6},{6,8},{8,10},{10,12},{12,14},{14,16},{16,18},{18... | collective-permute-start | bytes 12296 | tf_op jit(solution)/shard_map/ppermute | solution.py:274
  32.3 20.3 %collective-permute-start.4 = (bf16[4,1024,128]{2,1,0:T(8,128)(2,1)S(1)}, bf16[4,1024,128]{2,1,0:T(8,128)(2,1)}, u32[]{:S(2)}, u32[]{:S(2)}) collective-permute-start(bf16[4,1024,128]{2,1,0:T(8,128)(2,1)S(1)} %all-to-all-done.columns), channel_id=1, source_target_pairs={{0,64},{64,0},{128,192},{192,128},{256,320},{320,256},{384,448},{4... | collective-permute-start | bytes 3145736 | tf_op jit(solution)/shard_map/ppermute | solution.py:280
  34.9 28.5 %all-to-all-start.1 = ((f32[32,1,128]{2,1,0:T(1,128)}), f32[32,1,128]{2,1,0:T(1,128)S(1)}, u32[]{:S(2)}, u32[]{:S(2)}) async-start(f32[32,1,128]{2,1,0:T(1,128)} %bitcast.9), calls=%async_computation.1 | async-start | bytes 32768 | tf_op jit(solution)/shard_map/all_to_all | solution.py:279
  40.6 19.4 %collective-permute-start.2 = (f32[1,1024]{1,0:T(1,128)S(1)}, f32[1,1024]{1,0:T(1,128)S(1)}, u32[]{:S(2)}, u32[]{:S(2)}) collective-permute-start(f32[1,1024]{1,0:T(1,128)S(1)} %bitcast.26), channel_id=1, source_target_pairs={{1,0},{3,2},{5,4},{7,6},{9,8},{11,10},{13,12},{15,14},{17,16},{19,... | collective-permute-start | bytes 12296 | tf_op jit(solution)/shard_map/ppermute | solution.py:281
  52.5 1.0 %copy-start.2 = (bf16[1,256,1024]{2,1,0:T(8,128)(2,1)S(1)}, bf16[1,256,1024]{2,1,0:T(8,128)(2,1)}, u32[]{:S(2)}) copy-start(bf16[1,256,1024]{2,1,0:T(8,128)(2,1)} %param.6) | copy-start | bytes 1572868
  53.6 1.0 %copy-start.4 = (bf16[1,256,1024]{2,1,0:T(8,128)(2,1)S(1)}, bf16[1,256,1024]{2,1,0:T(8,128)(2,1)}, u32[]{:S(2)}) copy-start(bf16[1,256,1024]{2,1,0:T(8,128)(2,1)} %param.7) | copy-start | bytes 1572868
  63.5 5.4 %collective-permute-start.6 = (f32[1]{0:T(128)S(1)}, f32[1]{0:T(128)}, u32[]{:S(2)}, u32[]{:S(2)}) collective-permute-start(f32[1]{0:T(128)S(1)} %bitcast.31), channel_id=1, source_target_pairs={{0,1},{2,3},{4,5},{6,7},{8,9},{10,11},{12,13},{14,15},{16,17},{18,... | collective-permute-start | bytes 20 | tf_op jit(solution)/shard_map/ppermute | solution.py:285

commit v3 on v2

--- a/solution.py
+++ b/solution.py
@@ -13,7 +13,7 @@
 BF16 = jnp.bfloat16
 VMEM = pltpu.VMEM
 HBM = pltpu.HBM
-TOTAL_COST = pl.CostEstimate(flops=12 * 10**9, bytes_accessed=24 * 10**6, transcendentals=0)
+SPREAD_COST = pl.CostEstimate(flops=12 * 10**9, bytes_accessed=24 * 10**6, transcendentals=0)
 LIGHT = pl.CostEstimate(flops=1, bytes_accessed=1, transcendentals=0)
 
 
@@ -29,43 +29,55 @@
     return jnp.dot(a, b, preferred_element_type=F32)
 
 
-def edge_kernel(column_sums, row_sums, guess, emit, out):
+def edge_kernel(column_sums, guess, emit, out):
     row = lax.broadcasted_iota(jnp.int32, out.shape, 0)
-    sums = jnp.where(parity() == 0, column_sums[...], row_sums[...])
     rows = pltpu.roll(guess[...].astype(F32)[8:], 5, 0)
-    out[...] = jnp.where(row == 0, sums, jnp.where(row < 5, rows, emit[...].astype(F32)[8:]))
-
-
-def make_edge(column_sums, row_sums, guess_rows, emit_rows):
+    out[...] = jnp.where(row == 0, column_sums[...], jnp.where(row < 5, rows, emit[...].astype(F32)[8:]))
+
+
+def make_edge(column_sums, guess_rows, emit_rows):
     states = guess_rows.shape[1]
     last = guess_rows.shape[0] // EDGE - 1
     tail = pl.BlockSpec((EDGE, states), lambda i: (last, 0))
     return pl.pallas_call(
         edge_kernel,
         grid=(1,),
-        in_specs=[pl.BlockSpec((1, states), lambda i: (0, 0))] * 2 + [tail, tail],
+        in_specs=[pl.BlockSpec((1, states), lambda i: (0, 0)), tail, tail],
         out_specs=pl.BlockSpec((8, states), lambda i: (0, 0)),
         out_shape=jax.ShapeDtypeStruct((8, states), F32),
         compiler_params=params(),
         cost_estimate=LIGHT,
         name="edge",
-    )(column_sums, row_sums, guess_rows, emit_rows)
-
-
-def total_kernel(column_sums, before, order, totals):
-    value = jnp.sum(column_sums[...] * before[0:1], axis=1, keepdims=True)
-    totals[...] = jnp.broadcast_to(value, totals.shape)
-
-
-def pair_total(column_sums, before, peers, order):
+    )(column_sums, guess_rows, emit_rows)
+
+
+def total_kernel(before, row_sums, total):
+    value = jnp.sum(before[0:1] * row_sums[...], axis=1, keepdims=True)
+    total[...] = jnp.broadcast_to(value, total.shape)
+
+
+def pair_total(before, row_sums):
     return pl.pallas_call(
         total_kernel,
-        in_specs=[pl.BlockSpec(memory_space=VMEM)] * 2 + [pl.BlockSpec(memory_space=pl.ANY)],
+        out_shape=jax.ShapeDtypeStruct((8, 128), F32),
+        compiler_params=params(),
+        cost_estimate=LIGHT,
+        name="pair_total",
+    )(before, row_sums)
+
+
+def spread_kernel(total, out):
+    out[...] = jnp.broadcast_to(total[0:1, :], out.shape)
+
+
+def spread(total, peers):
+    return pl.pallas_call(
+        spread_kernel,
         out_shape=jax.ShapeDtypeStruct((peers, 128), F32),
         compiler_params=params(),
-        cost_estimate=TOTAL_COST,
-        name="pair_total",
-    )(column_sums, before, order)
+        cost_estimate=SPREAD_COST,
+        name="spread",
+    )(total)
 
 
 def copies_kernel(shard, out):
@@ -81,6 +93,22 @@
         cost_estimate=LIGHT,
         name="copies",
     )(shard)
+
+
+def rows_kernel(first, tile, *refs):
+    refs[-1][...] = tile[first:, :]
+
+
+def rows_after(tile, first, *order):
+    rows, states = tile.shape
+    return pl.pallas_call(
+        functools.partial(rows_kernel, first),
+        in_specs=[pl.BlockSpec(memory_space=VMEM)] + [pl.BlockSpec(memory_space=pl.ANY)] * len(order),
+        out_shape=jax.ShapeDtypeStruct((rows - first, states), BF16),
+        compiler_params=params(),
+        cost_estimate=LIGHT,
+        name="rows",
+    )(tile, *order)
 
 
 def sweep_kernel(
@@ -174,7 +202,7 @@
 
 
 def product_kernel(
-    own, lower, got, column_sums, sums_got, row_sums, before, order, out, token, right, total, result, load_sems, out_sems
+    own, column_sums, row_sums, before, lower, got, order, out, token, right, left, total, result, load_sems, out_sems
 ):
     states = own.shape[0]
     parts, depth, _ = right.shape
@@ -199,35 +227,45 @@
         ]
         for load in loads:
             load.start()
-        scale = (states * states) / jnp.sum(column_sums[...] * sums_got[...], axis=1, keepdims=True)
+        sums = column_sums[...]
+        high = sums.astype(BF16).astype(F32)
+        mid = (sums - high).astype(BF16).astype(F32)
+        row = lax.broadcasted_iota(jnp.int32, (EDGE, states), 0)
+        low = sums - high - mid
+        split = jnp.where(row == 0, high, jnp.where(row == 1, mid, jnp.where(row == 2, low, 0.0))).astype(BF16)
         for p in range(parts):
+            where = slice(p * depth, (p + 1) * depth)
             loads[p].wait()
-            block = matmul(own[:half, p * depth : (p + 1) * depth], right[p])
+            block = matmul(jnp.concatenate([own[:half, where], split[:, where]], axis=0), right[p])
             total[...] = block if p == 0 else total[...] + block
-        finish(scale)
+        pair = jnp.sum(jnp.sum(total[half:, :], axis=0, keepdims=True), axis=1, keepdims=True)
+        finish((states * states) / pair)
 
     @pl.when(jnp.logical_not(even))
     def _():
+        load = pltpu.make_async_copy(lower, left, load_sems.at[0])
+        load.start()
         scale = (states * states) / jnp.sum(row_sums[...] * before[0:1], axis=1, keepdims=True)
-        total[...] = matmul(lower[...], own[...])
+        load.wait()
+        total[:half, :] = matmul(left[...], own[...])
         finish(scale)
 
     for p in range(parts):
         store(p).wait()
 
 
-def pair_product(own, lower, got, column_sums, sums_got, row_sums, before, order):
+def pair_product(own, column_sums, row_sums, before, lower, got, order):
     states = own.shape[0]
     half, parts = states // 2, 4
-    spaces = (VMEM, VMEM, pl.ANY, VMEM, VMEM, VMEM, VMEM, pl.ANY)
     return pl.pallas_call(
         product_kernel,
-        in_specs=[pl.BlockSpec(memory_space=space) for space in spaces],
+        in_specs=[pl.BlockSpec(memory_space=VMEM)] * 4 + [pl.BlockSpec(memory_space=pl.ANY)] * 3,
         out_specs=[pl.BlockSpec(memory_space=HBM), pl.BlockSpec(memory_space=VMEM)],
         out_shape=(jax.ShapeDtypeStruct((half, states), BF16), jax.ShapeDtypeStruct((8, 128), F32)),
         scratch_shapes=[
             VMEM((parts, states // parts, states), BF16),
-            VMEM((half, states), F32),
+            VMEM((half, states), BF16),
+            VMEM((half + EDGE, states), F32),
             VMEM((half, states), BF16),
             pltpu.SemaphoreType.DMA((parts,)),
             pltpu.SemaphoreType.DMA((parts,)),
@@ -235,7 +273,7 @@
         compiler_params=params(),
         cost_estimate=LIGHT,
         name="pair_product",
-    )(own, lower, got, column_sums, sums_got, row_sums, before, order)
+    )(own, column_sums, row_sums, before, lower, got, order)
 
 
 def mean_kernel(states, totals, order, level):
@@ -271,16 +309,15 @@
     columns = lax.all_to_all(copies, "rec", 0, 0, tiled=True, axis_index_groups=cores)
     wide = tile.astype(F32)
     column_sums, row_sums = jnp.sum(wide, axis=0)[None], jnp.sum(wide, axis=1)[None]
-    pair_columns = lax.ppermute(column_sums, "tm", [(t, (t + 2) % size) for t in range(0, size, 2)])
-    edge = make_edge(column_sums, row_sums, guess[0], emission[0])
+    edge = make_edge(column_sums, guess[0], emission[0])
     before = lax.ppermute(edge, "tm", [(t, (t + 1) % size) for t in range(size)])
-    lower = lax.ppermute(tile[states // 2 :], "tm", over)
-    totals = pair_total(pair_columns, before, size // 2, lower)
+    lower = lax.ppermute(rows_after(tile, states // 2, before), "tm", over)
+    total = lax.ppermute(pair_total(before, row_sums), "tm", [(t, (t + 1) % size) for t in range(1, size, 2)])
+    totals = spread(total, size // 2)
     totals = lax.all_to_all(totals, ("rec", "tm"), 0, 0, tiled=True, axis_index_groups=peers)
     others = lax.ppermute(columns, "rec", [(r, r ^ 1) for r in range(recs)])
-    sums_got = lax.ppermute(row_sums, "tm", back)
     forward, frame_logscale, token = sweeps(before, guess[0], emission[0], start, columns, others)
-    combined, token = pair_product(tile, lower, got, column_sums, sums_got, row_sums, before, token)
+    combined, token = pair_product(tile, column_sums, row_sums, before, lower, got, token)
     level = mean_log(totals, states, token)[0, :1]
     told = lax.ppermute(level, "tm", over)
     return combined[None], jnp.where(even, level, told), forward[None], frame_logscale

time: 71.3 us -> 68.4 us (0.959)
  the two profiles are of different devices: /device:TPU:34 before, /device:TPU:32 now
where the time goes in v3:
time: 68.4 us; the launch traced here: 67.9 us
  starting transfers between devices  26.1 us (38%)
  waiting for transfers between devices  23.3 us (34%)
  Pallas kernels  11.6 us (17%)
  local copies, waits for them, and re-layouts  3.51 us (5%)
  between operations  2.6 us (4%)
  other arithmetic  0.72 us (1%)
    ppermute x1, waiting for transfers between devices, local(): lower = lax.ppermute(rows_after(tile, states // 2, before), 'tm', over)  12.4 us
    ppermute x1, starting transfers between devices, local(): got = lax.ppermute(tile, 'tm', back)  8.87 us
    ppermute x1, waiting for transfers between devices, local(): told = lax.ppermute(level, 'tm', over)  7.02 us
    pallas_call x1, Pallas kernels, sweeps(): pl.pallas_call(sweep_kernel, in_specs=[pl.BlockSpec(memory_space=VMEM)] *...  5.36 us
    all_to_all x1, starting transfers between devices, local(): lax.all_to_all(totals, ('rec', 'tm'), 0, 0, tiled=True, axis_index_groups...  5.29 us
    ppermute x1, waiting for transfers between devices, local(): lax.ppermute(edge, 'tm', [(t, (t + 1) % size) for t in range(size)])  3.88 us
    all_to_all x1, starting transfers between devices, local(): lax.all_to_all(copies, 'rec', 0, 0, tiled=True, axis_index_groups=cores)  3.51 us
    unnamed x14, local copies, waits for them, and re-layouts  3.51 us
  transfers between devices with their start and end apart: 8, of which 3 were waited for; matrix products, arithmetic and copies ran while one was open for 1% of the time, Pallas kernels for 17%

profile of v3, /device:TPU:32, one launch (start us, length us, event | category | flops | bytes accessed | tf_op | source)
XLA Modules:
  0.0 67.9 jit_solution(971202433785117235)
XLA Ops:
  0.6 8.9 %collective-permute-start.2 = (bf16[1024,1024]{1,0:T(8,128)(2,1)}, bf16[1024,1024]{1,0:T(8,128)(2,1)}, u32[]{:S(2)}, u32[]{:S(2)}) collective-permute-start(bf16[1024,1024]{1,0:T(8,128)(2,1)} %bitcast.16), channel_id=1, source_target_pairs={{1,0},{3,2},{5,4},{7,6},{9,8},{11,10},{13,12},{15,14},{17,16},{19,... | collective-permute-start | bytes 6291464 | tf_op jit(solution)/shard_map/ppermute | solution.py:307
  9.5 0.9 %copy-done.5 = bf16[1024,128]{1,0:T(8,128)(2,1)S(1)} copy-done((bf16[1024,128]{1,0:T(8,128)(2,1)S(1)}, bf16[1024,128]{1,0:T(8,128)(2,1)}, u32[]{:S(2)}) %copy-start.5) | copy-done | bytes 262168
  10.5 1.1 %copies.1 = bf16[4,1024,128]{2,1,0:T(8,128)(2,1)} custom-call(bf16[1024,128]{1,0:T(8,128)(2,1)S(1)} %copy-done.5), custom_call_target="tpu_custom_call" | custom-call | flops 1 | bytes 1 | tf_op jit(solution)/shard_map/copies/pallas_call | solution.py:89
  11.6 3.5 %all-to-all-start = ((bf16[4,1024,128]{2,1,0:T(8,128)(2,1)}), bf16[4,1024,128]{2,1,0:T(8,128)(2,1)S(1)}, u32[]{:S(2)}, u32[]{:S(2)}) async-start(bf16[4,1024,128]{2,1,0:T(8,128)(2,1)} %copies.1), calls=%async_computation | async-start | bytes 2097152 | tf_op jit(solution)/shard_map/all_to_all | solution.py:309
  15.1 0.0 copy-start.1
  15.1 0.7 %convert_reduce_fusion = (f32[1024]{0:T(1024)S(1)}, f32[1024]{0:T(1024)S(1)}) fusion(bf16[1,1,1024,1024]{3,2,1,0:T(8,128)(2,1)S(1)} %copy-done), kind=kLoop, calls=%fused_computation | loop fusion | flops 3143680 | bytes 2105344 | tf_op jit(solution)/shard_map/reduce_sum | solution.py:311
  15.8 0.3 copy-done.1
  16.1 0.2 copy-done.3
  16.3 1.9 %collective-permute-start = (f32[8,1024]{1,0:T(8,128)S(1)}, f32[8,1024]{1,0:T(8,128)S(1)}, u32[]{:S(2)}, u32[]{:S(2)}) collective-permute-start(f32[8,1024]{1,0:T(8,128)S(1)} %edge.1), channel_id=1, source_target_pairs={{0,1},{1,2},{2,3},{3,4},{4,5},{5,6},{6,7},{7,8},{8,9},{9,10},{10,1... | collective-permute-start | bytes 98312 | tf_op jit(solution)/shard_map/ppermute | solution.py:313
  18.2 3.9 %collective-permute-done.refs_0_.before = f32[8,1024]{1,0:T(8,128)S(1)} collective-permute-done((f32[8,1024]{1,0:T(8,128)S(1)}, f32[8,1024]{1,0:T(8,128)S(1)}, u32[]{:S(2)}, u32[]{:S(2)}) %collective-permute-start) | collective-permute-done | bytes 32800 | tf_op jit(solution)/shard_map/ppermute | solution.py:313
  22.1 0.1 pair_total.1
  22.2 1.9 %collective-permute-start.4 = (f32[8,128]{1,0:T(8,128)S(1)}, f32[8,128]{1,0:T(8,128)S(1)}, u32[]{:S(2)}, u32[]{:S(2)}) collective-permute-start(f32[8,128]{1,0:T(8,128)S(1)} %pair_total.1), channel_id=1, source_target_pairs={{1,2},{3,4},{5,6},{7,8},{9,10},{11,12},{13,14},{15,16},{17,18},{19... | collective-permute-start | bytes 12296 | tf_op jit(solution)/shard_map/ppermute | solution.py:315
  24.1 1.0 %rows.1 = bf16[512,1024]{1,0:T(8,128)(2,1)} custom-call(bf16[1024,1024]{1,0:T(8,128)(2,1)S(1)} %bitcast.17, f32[8,1024]{1,0:T(8,128)S(1)} %collective-permute-done.refs_0_.before), custom_call_target="tpu_custom_call" | custom-call | flops 1 | bytes 1 | tf_op jit(solution)/shard_map/rows/pallas_call | solution.py:104
  25.2 1.4 %collective-permute-start.1 = (bf16[512,1024]{1,0:T(8,128)(2,1)}, bf16[512,1024]{1,0:T(8,128)(2,1)}, u32[]{:S(2)}, u32[]{:S(2)}) collective-permute-start(bf16[512,1024]{1,0:T(8,128)(2,1)} %rows.1), channel_id=1, source_target_pairs={{0,1},{2,3},{4,5},{6,7},{8,9},{10,11},{12,13},{14,15},{16,17},{18,... | collective-permute-start | bytes 3145736 | tf_op jit(solution)/shard_map/ppermute | solution.py:314
  26.6 1.9 %collective-permute-start.3 = (bf16[4,1024,128]{2,1,0:T(8,128)(2,1)S(1)}, bf16[4,1024,128]{2,1,0:T(8,128)(2,1)}, u32[]{:S(2)}, u32[]{:S(2)}) collective-permute-start(bf16[4,1024,128]{2,1,0:T(8,128)(2,1)S(1)} %all-to-all-done.columns), channel_id=1, source_target_pairs={{0,64},{64,0},{128,192},{192,128},{256,320},{320,256},{384,448},{4... | collective-permute-start | bytes 3145736 | tf_op jit(solution)/shard_map/ppermute | solution.py:318
  28.5 0.6 spread.1
  29.1 5.3 %all-to-all-start.1 = ((f32[32,1,128]{2,1,0:T(1,128)}), f32[32,1,128]{2,1,0:T(1,128)S(1)}, u32[]{:S(2)}, u32[]{:S(2)}) async-start(f32[32,1,128]{2,1,0:T(1,128)} %bitcast.8), calls=%async_computation.1 | async-start | bytes 32768 | tf_op jit(solution)/shard_map/all_to_all | solution.py:317
  34.5 1.0 %copy-done.2 = bf16[1,256,1024]{2,1,0:T(8,128)(2,1)S(1)} copy-done((bf16[1,256,1024]{2,1,0:T(8,128)(2,1)S(1)}, bf16[1,256,1024]{2,1,0:T(8,128)(2,1)}, u32[]{:S(2)}) %copy-start.2) | copy-done | bytes 524312
  35.5 1.0 %copy-done.4 = bf16[1,256,1024]{2,1,0:T(8,128)(2,1)S(1)} copy-done((bf16[1,256,1024]{2,1,0:T(8,128)(2,1)S(1)}, bf16[1,256,1024]{2,1,0:T(8,128)(2,1)}, u32[]{:S(2)}) %copy-start.4) | copy-done | bytes 524312
  36.6 5.4 %sweeps.1 = (bf16[256,1024]{1,0:T(8,128)(2,1)}, f32[1,256]{1,0:T(1,128)}, f32[8,128]{1,0:T(8,128)S(1)}) custom-call(f32[8,1024]{1,0:T(8,128)S(1)} %collective-permute-done.refs_0_.before, bf16[1,1024]{1,0:T(2,128)(2,1)S(1)} %copy-done.6, bf16[256,1024]{1,0:T(8,128)(2,1)S(1)} %bitcast.20, bf16[256,1024]{1,0:T(8,128)(2,1)S(1)} %bitcast.22, ...), custom_call_target="tpu_custom_call" | custom-call | flops 1 | bytes 1 | tf_op jit(solution)/shard_map/sweeps/pallas_call | solution.py:182
  41.9 12.4 %collective-permute-done.1.lower = bf16[512,1024]{1,0:T(8,128)(2,1)} collective-permute-done((bf16[512,1024]{1,0:T(8,128)(2,1)}, bf16[512,1024]{1,0:T(8,128)(2,1)}, u32[]{:S(2)}, u32[]{:S(2)}) %collective-permute-start.1) | collective-permute-done | bytes 1048608 | tf_op jit(solution)/shard_map/ppermute | solution.py:314
  54.3 3.4 %pair_product.1 = (bf16[512,1024]{1,0:T(8,128)(2,1)}, f32[8,128]{1,0:T(8,128)S(1)}) custom-call(bf16[1024,1024]{1,0:T(8,128)(2,1)S(1)} %bitcast.18, f32[1,1024]{1,0:T(1,128)S(1)} %bitcast.25, f32[1,1024]{1,0:T(1,128)S(1)} %bitcast.27, f32[8,1024]{1,0:T(8,128)S(1)} %collective-permute-done.refs_0_.before, bf16[512,1024]{1,0:T(8,128)(2,1)} %collective-permute-done.1.lower, ...), custom_call_target="tpu_custom_call" | custom-call | flops 1 | bytes 1 | tf_op jit(solution)/shard_map/pair_product/pallas_call | solution.py:260
  57.8 1.3 %collective-permute-start.5 = (f32[1]{0:T(128)S(1)}, f32[1]{0:T(128)}, u32[]{:S(2)}, u32[]{:S(2)}) collective-permute-start(f32[1]{0:T(128)S(1)} %bitcast.28), channel_id=1, source_target_pairs={{0,1},{2,3},{4,5},{6,7},{8,9},{10,11},{12,13},{14,15},{16,17},{18,... | collective-permute-start | bytes 20 | tf_op jit(solution)/shard_map/ppermute | solution.py:322
  59.1 7.0 %collective-permute-done.5 = f32[1]{0:T(128)} collective-permute-done((f32[1]{0:T(128)S(1)}, f32[1]{0:T(128)}, u32[]{:S(2)}, u32[]{:S(2)}) %collective-permute-start.5) | collective-permute-done | bytes 36 | tf_op jit(solution)/shard_map/ppermute | solution.py:322
  (15 shorter events, 0.1 us)
Async XLA Ops:
  0.6 14.5 %copy-start = (bf16[1,1,1024,1024]{3,2,1,0:T(8,128)(2,1)S(1)}, bf16[1,1,1024,1024]{3,2,1,0:T(8,128)(2,1)}, u32[]{:S(2)}) copy-start(bf16[1,1,1024,1024]{3,2,1,0:T(8,128)(2,1)} %param.5) | copy-start | bytes 6291460
  0.6 53.7 %collective-permute-start.2 = (bf16[1024,1024]{1,0:T(8,128)(2,1)}, bf16[1024,1024]{1,0:T(8,128)(2,1)}, u32[]{:S(2)}, u32[]{:S(2)}) collective-permute-start(bf16[1024,1024]{1,0:T(8,128)(2,1)} %bitcast.16), channel_id=1, source_target_pairs={{1,0},{3,2},{5,4},{7,6},{9,8},{11,10},{13,12},{15,14},{17,16},{19,... | collective-permute-start | bytes 6291464 | tf_op jit(solution)/shard_map/ppermute | solution.py:307
  9.5 0.9 %copy-start.5 = (bf16[1024,128]{1,0:T(8,128)(2,1)S(1)}, bf16[1024,128]{1,0:T(8,128)(2,1)}, u32[]{:S(2)}) copy-start(bf16[1024,128]{1,0:T(8,128)(2,1)} %shard.1) | copy-start | bytes 786436
  11.6 15.0 %all-to-all-start = ((bf16[4,1024,128]{2,1,0:T(8,128)(2,1)}), bf16[4,1024,128]{2,1,0:T(8,128)(2,1)S(1)}, u32[]{:S(2)}, u32[]{:S(2)}) async-start(bf16[4,1024,128]{2,1,0:T(8,128)(2,1)} %copies.1), calls=%async_computation | async-start | bytes 2097152 | tf_op jit(solution)/shard_map/all_to_all | solution.py:309
  15.1 1.0 %copy-start.1 = (bf16[1,256,1024]{2,1,0:T(8,128)(2,1)S(1)}, bf16[1,256,1024]{2,1,0:T(8,128)(2,1)}, u32[]{:S(2)}) copy-start(bf16[1,256,1024]{2,1,0:T(8,128)(2,1)} %param.6) | copy-start | bytes 1572868
  15.1 1.2 %copy-start.3 = (bf16[1,256,1024]{2,1,0:T(8,128)(2,1)S(1)}, bf16[1,256,1024]{2,1,0:T(8,128)(2,1)}, u32[]{:S(2)}) copy-start(bf16[1,256,1024]{2,1,0:T(8,128)(2,1)} %param.7) | copy-start | bytes 1572868
  16.3 5.8 %collective-permute-start = (f32[8,1024]{1,0:T(8,128)S(1)}, f32[8,1024]{1,0:T(8,128)S(1)}, u32[]{:S(2)}, u32[]{:S(2)}) collective-permute-start(f32[8,1024]{1,0:T(8,128)S(1)} %edge.1), channel_id=1, source_target_pairs={{0,1},{1,2},{2,3},{3,4},{4,5},{5,6},{6,7},{7,8},{8,9},{9,10},{10,1... | collective-permute-start | bytes 98312 | tf_op jit(solution)/shard_map/ppermute | solution.py:313
  22.2 6.3 %collective-permute-start.4 = (f32[8,128]{1,0:T(8,128)S(1)}, f32[8,128]{1,0:T(8,128)S(1)}, u32[]{:S(2)}, u32[]{:S(2)}) collective-permute-start(f32[8,128]{1,0:T(8,128)S(1)} %pair_total.1), channel_id=1, source_target_pairs={{1,2},{3,4},{5,6},{7,8},{9,10},{11,12},{13,14},{15,16},{17,18},{19... | collective-permute-start | bytes 12296 | tf_op jit(solution)/shard_map/ppermute | solution.py:315
  25.2 9.3 %copy-start.6 = (bf16[1,1024]{1,0:T(2,128)(2,1)S(1)}, bf16[1,1024]{1,0:T(2,128)(2,1)}, u32[]{:S(2)}) copy-start(bf16[1,1024]{1,0:T(2,128)(2,1)} %start.1) | copy-start | bytes 6148
  25.2 29.1 %collective-permute-start.1 = (bf16[512,1024]{1,0:T(8,128)(2,1)}, bf16[512,1024]{1,0:T(8,128)(2,1)}, u32[]{:S(2)}, u32[]{:S(2)}) collective-permute-start(bf16[512,1024]{1,0:T(8,128)(2,1)} %rows.1), channel_id=1, source_target_pairs={{0,1},{2,3},{4,5},{6,7},{8,9},{10,11},{12,13},{14,15},{16,17},{18,... | collective-permute-start | bytes 3145736 | tf_op jit(solution)/shard_map/ppermute | solution.py:314
  26.6 7.9 %collective-permute-start.3 = (bf16[4,1024,128]{2,1,0:T(8,128)(2,1)S(1)}, bf16[4,1024,128]{2,1,0:T(8,128)(2,1)}, u32[]{:S(2)}, u32[]{:S(2)}) collective-permute-start(bf16[4,1024,128]{2,1,0:T(8,128)(2,1)S(1)} %all-to-all-done.columns), channel_id=1, source_target_pairs={{0,64},{64,0},{128,192},{192,128},{256,320},{320,256},{384,448},{4... | collective-permute-start | bytes 3145736 | tf_op jit(solution)/shard_map/ppermute | solution.py:318
  29.1 28.6 %all-to-all-start.1 = ((f32[32,1,128]{2,1,0:T(1,128)}), f32[32,1,128]{2,1,0:T(1,128)S(1)}, u32[]{:S(2)}, u32[]{:S(2)}) async-start(f32[32,1,128]{2,1,0:T(1,128)} %bitcast.8), calls=%async_computation.1 | async-start | bytes 32768 | tf_op jit(solution)/shard_map/all_to_all | solution.py:317
  34.5 1.0 %copy-start.2 = (bf16[1,256,1024]{2,1,0:T(8,128)(2,1)S(1)}, bf16[1,256,1024]{2,1,0:T(8,128)(2,1)}, u32[]{:S(2)}) copy-start(bf16[1,256,1024]{2,1,0:T(8,128)(2,1)} %param.6) | copy-start | bytes 1572868
  35.5 1.0 %copy-start.4 = (bf16[1,256,1024]{2,1,0:T(8,128)(2,1)S(1)}, bf16[1,256,1024]{2,1,0:T(8,128)(2,1)}, u32[]{:S(2)}) copy-start(bf16[1,256,1024]{2,1,0:T(8,128)(2,1)} %param.7) | copy-start | bytes 1572868
  57.8 8.3 %collective-permute-start.5 = (f32[1]{0:T(128)S(1)}, f32[1]{0:T(128)}, u32[]{:S(2)}, u32[]{:S(2)}) collective-permute-start(f32[1]{0:T(128)S(1)} %bitcast.28), channel_id=1, source_target_pairs={{0,1},{2,3},{4,5},{6,7},{8,9},{10,11},{12,13},{14,15},{16,17},{18,... | collective-permute-start | bytes 20 | tf_op jit(solution)/shard_map/ppermute | solution.py:322

commit v4 on v3

--- a/solution.py
+++ b/solution.py
@@ -95,20 +95,42 @@
     )(shard)
 
 
-def rows_kernel(first, tile, *refs):
-    refs[-1][...] = tile[first:, :]
-
-
-def rows_after(tile, first, *order):
-    rows, states = tile.shape
-    return pl.pallas_call(
-        functools.partial(rows_kernel, first),
-        in_specs=[pl.BlockSpec(memory_space=VMEM)] + [pl.BlockSpec(memory_space=pl.ANY)] * len(order),
-        out_shape=jax.ShapeDtypeStruct((rows - first, states), BF16),
+def rows_kernel(tile, order, out, held, sems, out_sems):
+    parts, rows, _ = held.shape
+    first = tile.shape[0] - parts * rows
+    loads = [
+        pltpu.make_async_copy(tile.at[pl.ds(first + p * rows, rows), :], held.at[p], sems.at[p]) for p in range(parts)
+    ]
+    stores = [pltpu.make_async_copy(held.at[p], out.at[pl.ds(p * rows, rows), :], out_sems.at[p]) for p in range(parts)]
+
+    @pl.when(parity() == 0)
+    def _():
+        for load in loads:
+            load.start()
+        for load, store in zip(loads, stores):
+            load.wait()
+            store.start()
+        for store in stores:
+            store.wait()
+
+
+def rows_after(tile, first, order):
+    rows, states = tile.shape[0] - first, tile.shape[1]
+    parts = 4
+    return pl.pallas_call(
+        rows_kernel,
+        in_specs=[pl.BlockSpec(memory_space=HBM), pl.BlockSpec(memory_space=pl.ANY)],
+        out_specs=pl.BlockSpec(memory_space=HBM),
+        out_shape=jax.ShapeDtypeStruct((rows, states), BF16),
+        scratch_shapes=[
+            VMEM((parts, rows // parts, states), BF16),
+            pltpu.SemaphoreType.DMA((parts,)),
+            pltpu.SemaphoreType.DMA((parts,)),
+        ],
         compiler_params=params(),
         cost_estimate=LIGHT,
         name="rows",
-    )(tile, *order)
+    )(tile, order)
 
 
 def sweep_kernel(

time: 68.4 us -> 67.4 us (0.985)
  Pallas kernels: 11.6 us -> 10.7 us
    ppermute x1, waiting for transfers between devices: 7.02 us -> 5.88 us  [local(): told = lax.ppermute(level, 'tm', over)]
    ppermute x1, waiting for transfers between devices: 12.4 us -> 13.5 us  [local(): lower = lax.ppermute(rows_after(tile, states // 2, before), 'tm', over)]
    pallas_call x1, Pallas kernels: 1.04 us -> 0.09 us  [rows_after(): pl.pallas_call(rows_kernel, in_specs=[pl.BlockSpec(memory_space=HBM), pl....]
  transfers between devices with their start and end apart: 8 -> 8, of which waited for: 3 -> 4; matrix products, arithmetic and copies ran while one was open for 1% -> 1% of each run, Pallas kernels for 17% -> 16%
where the time goes in v4:
time: 67.4 us; the launch traced here: 66.8 us
  starting transfers between devices  25.6 us (38%)
  waiting for transfers between devices  23.7 us (35%)
  Pallas kernels  10.7 us (16%)
  local copies, waits for them, and re-layouts  3.51 us (5%)
  between operations  2.61 us (4%)
  other arithmetic  0.72 us (1%)
    ppermute x1, waiting for transfers between devices, local(): lower = lax.ppermute(rows_after(tile, states // 2, before), 'tm', over)  13.5 us
    ppermute x1, starting transfers between devices, local(): got = lax.ppermute(tile, 'tm', back)  8.87 us
    ppermute x1, waiting for transfers between devices, local(): told = lax.ppermute(level, 'tm', over)  5.88 us
    pallas_call x1, Pallas kernels, sweeps(): pl.pallas_call(sweep_kernel, in_specs=[pl.BlockSpec(memory_space=VMEM)] *...  5.35 us
    all_to_all x1, starting transfers between devices, local(): lax.all_to_all(totals, ('rec', 'tm'), 0, 0, tiled=True, axis_index_groups...  4.92 us
    ppermute x1, waiting for transfers between devices, local(): lax.ppermute(edge, 'tm', [(t, (t + 1) % size) for t in range(size)])  3.88 us
    all_to_all x1, starting transfers between devices, local(): lax.all_to_all(copies, 'rec', 0, 0, tiled=True, axis_index_groups=cores)  3.51 us
    unnamed x14, local copies, waits for them, and re-layouts  3.51 us
  transfers between devices with their start and end apart: 8, of which 4 were waited for; matrix products, arithmetic and copies ran while one was open for 1% of the time, Pallas kernels for 16%

profile of v4, /device:TPU:32, one launch (start us, length us, event | category | flops | bytes accessed | tf_op | source)
XLA Modules:
  0.0 66.8 jit_solution(8820026129006608017)
XLA Ops:
  0.6 8.9 %collective-permute-start.2 = (bf16[1024,1024]{1,0:T(8,128)(2,1)}, bf16[1024,1024]{1,0:T(8,128)(2,1)}, u32[]{:S(2)}, u32[]{:S(2)}) collective-permute-start(bf16[1024,1024]{1,0:T(8,128)(2,1)} %bitcast.16), channel_id=1, source_target_pairs={{1,0},{3,2},{5,4},{7,6},{9,8},{11,10},{13,12},{15,14},{17,16},{19,... | collective-permute-start | bytes 6291464 | tf_op jit(solution)/shard_map/ppermute | solution.py:329
  9.5 0.9 %copy-done.5 = bf16[1024,128]{1,0:T(8,128)(2,1)S(1)} copy-done((bf16[1024,128]{1,0:T(8,128)(2,1)S(1)}, bf16[1024,128]{1,0:T(8,128)(2,1)}, u32[]{:S(2)}) %copy-start.5) | copy-done | bytes 262168
  10.5 1.1 %copies.1 = bf16[4,1024,128]{2,1,0:T(8,128)(2,1)} custom-call(bf16[1024,128]{1,0:T(8,128)(2,1)S(1)} %copy-done.5), custom_call_target="tpu_custom_call" | custom-call | flops 1 | bytes 1 | tf_op jit(solution)/shard_map/copies/pallas_call | solution.py:89
  11.6 3.5 %all-to-all-start = ((bf16[4,1024,128]{2,1,0:T(8,128)(2,1)}), bf16[4,1024,128]{2,1,0:T(8,128)(2,1)S(1)}, u32[]{:S(2)}, u32[]{:S(2)}) async-start(bf16[4,1024,128]{2,1,0:T(8,128)(2,1)} %copies.1), calls=%async_computation | async-start | bytes 2097152 | tf_op jit(solution)/shard_map/all_to_all | solution.py:331
  15.1 0.7 %convert_reduce_fusion = (f32[1024]{0:T(1024)S(1)}, f32[1024]{0:T(1024)S(1)}) fusion(bf16[1,1,1024,1024]{3,2,1,0:T(8,128)(2,1)S(1)} %copy-done), kind=kLoop, calls=%fused_computation | loop fusion | flops 3143680 | bytes 2105344 | tf_op jit(solution)/shard_map/reduce_sum | solution.py:333
  15.8 0.3 copy-done.1
  16.1 0.2 copy-done.3
  16.3 1.9 %collective-permute-start = (f32[8,1024]{1,0:T(8,128)S(1)}, f32[8,1024]{1,0:T(8,128)S(1)}, u32[]{:S(2)}, u32[]{:S(2)}) collective-permute-start(f32[8,1024]{1,0:T(8,128)S(1)} %edge.1), channel_id=1, source_target_pairs={{0,1},{1,2},{2,3},{3,4},{4,5},{5,6},{6,7},{7,8},{8,9},{9,10},{10,1... | collective-permute-start | bytes 98312 | tf_op jit(solution)/shard_map/ppermute | solution.py:335
  18.2 3.9 %collective-permute-done.order.before = f32[8,1024]{1,0:T(8,128)S(1)} collective-permute-done((f32[8,1024]{1,0:T(8,128)S(1)}, f32[8,1024]{1,0:T(8,128)S(1)}, u32[]{:S(2)}, u32[]{:S(2)}) %collective-permute-start) | collective-permute-done | bytes 32800 | tf_op jit(solution)/shard_map/ppermute | solution.py:335
  22.1 0.1 pair_total.1
  22.2 1.9 %collective-permute-start.4 = (f32[8,128]{1,0:T(8,128)S(1)}, f32[8,128]{1,0:T(8,128)S(1)}, u32[]{:S(2)}, u32[]{:S(2)}) collective-permute-start(f32[8,128]{1,0:T(8,128)S(1)} %pair_total.1), channel_id=1, source_target_pairs={{1,2},{3,4},{5,6},{7,8},{9,10},{11,12},{13,14},{15,16},{17,18},{19... | collective-permute-start | bytes 12296 | tf_op jit(solution)/shard_map/ppermute | solution.py:337
  24.1 0.1 rows.1
  24.2 1.3 %collective-permute-start.1 = (bf16[512,1024]{1,0:T(8,128)(2,1)}, bf16[512,1024]{1,0:T(8,128)(2,1)}, u32[]{:S(2)}, u32[]{:S(2)}) collective-permute-start(bf16[512,1024]{1,0:T(8,128)(2,1)} %rows.1), channel_id=1, source_target_pairs={{0,1},{2,3},{4,5},{6,7},{8,9},{10,11},{12,13},{14,15},{16,17},{18,... | collective-permute-start | bytes 3145736 | tf_op jit(solution)/shard_map/ppermute | solution.py:336
  25.5 0.4 all-to-all-done.columns
  25.9 1.9 %collective-permute-start.3 = (bf16[4,1024,128]{2,1,0:T(8,128)(2,1)S(1)}, bf16[4,1024,128]{2,1,0:T(8,128)(2,1)}, u32[]{:S(2)}, u32[]{:S(2)}) collective-permute-start(bf16[4,1024,128]{2,1,0:T(8,128)(2,1)S(1)} %all-to-all-done.columns), channel_id=1, source_target_pairs={{0,64},{64,0},{128,192},{192,128},{256,320},{320,256},{384,448},{4... | collective-permute-start | bytes 3145736 | tf_op jit(solution)/shard_map/ppermute | solution.py:340
  27.9 0.6 spread.1
  28.5 4.9 %all-to-all-start.1 = ((f32[32,1,128]{2,1,0:T(1,128)}), f32[32,1,128]{2,1,0:T(1,128)S(1)}, u32[]{:S(2)}, u32[]{:S(2)}) async-start(f32[32,1,128]{2,1,0:T(1,128)} %bitcast.8), calls=%async_computation.1 | async-start | bytes 32768 | tf_op jit(solution)/shard_map/all_to_all | solution.py:339
  33.5 1.0 %copy-done.2 = bf16[1,256,1024]{2,1,0:T(8,128)(2,1)S(1)} copy-done((bf16[1,256,1024]{2,1,0:T(8,128)(2,1)S(1)}, bf16[1,256,1024]{2,1,0:T(8,128)(2,1)}, u32[]{:S(2)}) %copy-start.2) | copy-done | bytes 524312
  34.5 1.0 %copy-done.4 = bf16[1,256,1024]{2,1,0:T(8,128)(2,1)S(1)} copy-done((bf16[1,256,1024]{2,1,0:T(8,128)(2,1)S(1)}, bf16[1,256,1024]{2,1,0:T(8,128)(2,1)}, u32[]{:S(2)}) %copy-start.4) | copy-done | bytes 524312
  35.5 5.4 %sweeps.1 = (bf16[256,1024]{1,0:T(8,128)(2,1)}, f32[1,256]{1,0:T(1,128)}, f32[8,128]{1,0:T(8,128)S(1)}) custom-call(f32[8,1024]{1,0:T(8,128)S(1)} %collective-permute-done.order.before, bf16[1,1024]{1,0:T(2,128)(2,1)S(1)} %copy-done.6, bf16[256,1024]{1,0:T(8,128)(2,1)S(1)} %bitcast.20, bf16[256,1024]{1,0:T(8,128)(2,1)S(1)} %bitcast.22, ...), custom_call_target="tpu_custom_call" | custom-call | flops 1 | bytes 1 | tf_op jit(solution)/shard_map/sweeps/pallas_call | solution.py:204
  40.9 13.5 %collective-permute-done.1.lower = bf16[512,1024]{1,0:T(8,128)(2,1)} collective-permute-done((bf16[512,1024]{1,0:T(8,128)(2,1)}, bf16[512,1024]{1,0:T(8,128)(2,1)}, u32[]{:S(2)}, u32[]{:S(2)}) %collective-permute-start.1) | collective-permute-done | bytes 1048608 | tf_op jit(solution)/shard_map/ppermute | solution.py:336
  54.4 3.4 %pair_product.1 = (bf16[512,1024]{1,0:T(8,128)(2,1)}, f32[8,128]{1,0:T(8,128)S(1)}) custom-call(bf16[1024,1024]{1,0:T(8,128)(2,1)S(1)} %bitcast.18, f32[1,1024]{1,0:T(1,128)S(1)} %bitcast.25, f32[1,1024]{1,0:T(1,128)S(1)} %bitcast.27, f32[8,1024]{1,0:T(8,128)S(1)} %collective-permute-done.order.before, bf16[512,1024]{1,0:T(8,128)(2,1)} %collective-permute-done.1.lower, ...), custom_call_target="tpu_custom_call" | custom-call | flops 1 | bytes 1 | tf_op jit(solution)/shard_map/pair_product/pallas_call | solution.py:282
  57.8 1.3 %collective-permute-start.5 = (f32[1]{0:T(128)S(1)}, f32[1]{0:T(128)}, u32[]{:S(2)}, u32[]{:S(2)}) collective-permute-start(f32[1]{0:T(128)S(1)} %bitcast.28), channel_id=1, source_target_pairs={{0,1},{2,3},{4,5},{6,7},{8,9},{10,11},{12,13},{14,15},{16,17},{18,... | collective-permute-start | bytes 20 | tf_op jit(solution)/shard_map/ppermute | solution.py:344
  59.1 5.9 %collective-permute-done.5 = f32[1]{0:T(128)} collective-permute-done((f32[1]{0:T(128)S(1)}, f32[1]{0:T(128)}, u32[]{:S(2)}, u32[]{:S(2)}) %collective-permute-start.5) | collective-permute-done | bytes 36 | tf_op jit(solution)/shard_map/ppermute | solution.py:344
  (15 shorter events, 0.1 us)
Async XLA Ops:
  0.6 14.5 %copy-start = (bf16[1,1,1024,1024]{3,2,1,0:T(8,128)(2,1)S(1)}, bf16[1,1,1024,1024]{3,2,1,0:T(8,128)(2,1)}, u32[]{:S(2)}) copy-start(bf16[1,1,1024,1024]{3,2,1,0:T(8,128)(2,1)} %param.5) | copy-start | bytes 6291460
  0.6 53.8 %collective-permute-start.2 = (bf16[1024,1024]{1,0:T(8,128)(2,1)}, bf16[1024,1024]{1,0:T(8,128)(2,1)}, u32[]{:S(2)}, u32[]{:S(2)}) collective-permute-start(bf16[1024,1024]{1,0:T(8,128)(2,1)} %bitcast.16), channel_id=1, source_target_pairs={{1,0},{3,2},{5,4},{7,6},{9,8},{11,10},{13,12},{15,14},{17,16},{19,... | collective-permute-start | bytes 6291464 | tf_op jit(solution)/shard_map/ppermute | solution.py:329
  9.5 0.9 %copy-start.5 = (bf16[1024,128]{1,0:T(8,128)(2,1)S(1)}, bf16[1024,128]{1,0:T(8,128)(2,1)}, u32[]{:S(2)}) copy-start(bf16[1024,128]{1,0:T(8,128)(2,1)} %shard.1) | copy-start | bytes 786436
  11.6 14.4 %all-to-all-start = ((bf16[4,1024,128]{2,1,0:T(8,128)(2,1)}), bf16[4,1024,128]{2,1,0:T(8,128)(2,1)S(1)}, u32[]{:S(2)}, u32[]{:S(2)}) async-start(bf16[4,1024,128]{2,1,0:T(8,128)(2,1)} %copies.1), calls=%async_computation | async-start | bytes 2097152 | tf_op jit(solution)/shard_map/all_to_all | solution.py:331
  15.1 1.0 %copy-start.1 = (bf16[1,256,1024]{2,1,0:T(8,128)(2,1)S(1)}, bf16[1,256,1024]{2,1,0:T(8,128)(2,1)}, u32[]{:S(2)}) copy-start(bf16[1,256,1024]{2,1,0:T(8,128)(2,1)} %param.6) | copy-start | bytes 1572868
  15.1 1.2 %copy-start.3 = (bf16[1,256,1024]{2,1,0:T(8,128)(2,1)S(1)}, bf16[1,256,1024]{2,1,0:T(8,128)(2,1)}, u32[]{:S(2)}) copy-start(bf16[1,256,1024]{2,1,0:T(8,128)(2,1)} %param.7) | copy-start | bytes 1572868
  16.3 5.8 %collective-permute-start = (f32[8,1024]{1,0:T(8,128)S(1)}, f32[8,1024]{1,0:T(8,128)S(1)}, u32[]{:S(2)}, u32[]{:S(2)}) collective-permute-start(f32[8,1024]{1,0:T(8,128)S(1)} %edge.1), channel_id=1, source_target_pairs={{0,1},{1,2},{2,3},{3,4},{4,5},{5,6},{6,7},{7,8},{8,9},{9,10},{10,1... | collective-permute-start | bytes 98312 | tf_op jit(solution)/shard_map/ppermute | solution.py:335
  22.2 5.7 %collective-permute-start.4 = (f32[8,128]{1,0:T(8,128)S(1)}, f32[8,128]{1,0:T(8,128)S(1)}, u32[]{:S(2)}, u32[]{:S(2)}) collective-permute-start(f32[8,128]{1,0:T(8,128)S(1)} %pair_total.1), channel_id=1, source_target_pairs={{1,2},{3,4},{5,6},{7,8},{9,10},{11,12},{13,14},{15,16},{17,18},{19... | collective-permute-start | bytes 12296 | tf_op jit(solution)/shard_map/ppermute | solution.py:337
  24.2 9.2 %copy-start.6 = (bf16[1,1024]{1,0:T(2,128)(2,1)S(1)}, bf16[1,1024]{1,0:T(2,128)(2,1)}, u32[]{:S(2)}) copy-start(bf16[1,1024]{1,0:T(2,128)(2,1)} %start.1) | copy-start | bytes 6148
  24.2 30.2 %collective-permute-start.1 = (bf16[512,1024]{1,0:T(8,128)(2,1)}, bf16[512,1024]{1,0:T(8,128)(2,1)}, u32[]{:S(2)}, u32[]{:S(2)}) collective-permute-start(bf16[512,1024]{1,0:T(8,128)(2,1)} %rows.1), channel_id=1, source_target_pairs={{0,1},{2,3},{4,5},{6,7},{8,9},{10,11},{12,13},{14,15},{16,17},{18,... | collective-permute-start | bytes 3145736 | tf_op jit(solution)/shard_map/ppermute | solution.py:336
  25.9 7.5 %collective-permute-start.3 = (bf16[4,1024,128]{2,1,0:T(8,128)(2,1)S(1)}, bf16[4,1024,128]{2,1,0:T(8,128)(2,1)}, u32[]{:S(2)}, u32[]{:S(2)}) collective-permute-start(bf16[4,1024,128]{2,1,0:T(8,128)(2,1)S(1)} %all-to-all-done.columns), channel_id=1, source_target_pairs={{0,64},{64,0},{128,192},{192,128},{256,320},{320,256},{384,448},{4... | collective-permute-start | bytes 3145736 | tf_op jit(solution)/shard_map/ppermute | solution.py:340
  28.5 29.3 %all-to-all-start.1 = ((f32[32,1,128]{2,1,0:T(1,128)}), f32[32,1,128]{2,1,0:T(1,128)S(1)}, u32[]{:S(2)}, u32[]{:S(2)}) async-start(f32[32,1,128]{2,1,0:T(1,128)} %bitcast.8), calls=%async_computation.1 | async-start | bytes 32768 | tf_op jit(solution)/shard_map/all_to_all | solution.py:339
  33.4 1.0 %copy-start.2 = (bf16[1,256,1024]{2,1,0:T(8,128)(2,1)S(1)}, bf16[1,256,1024]{2,1,0:T(8,128)(2,1)}, u32[]{:S(2)}) copy-start(bf16[1,256,1024]{2,1,0:T(8,128)(2,1)} %param.6) | copy-start | bytes 1572868
  34.5 1.0 %copy-start.4 = (bf16[1,256,1024]{2,1,0:T(8,128)(2,1)S(1)}, bf16[1,256,1024]{2,1,0:T(8,128)(2,1)}, u32[]{:S(2)}) copy-start(bf16[1,256,1024]{2,1,0:T(8,128)(2,1)} %param.7) | copy-start | bytes 1572868
  57.8 7.2 %collective-permute-start.5 = (f32[1]{0:T(128)S(1)}, f32[1]{0:T(128)}, u32[]{:S(2)}, u32[]{:S(2)}) collective-permute-start(f32[1]{0:T(128)S(1)} %bitcast.28), channel_id=1, source_target_pairs={{0,1},{2,3},{4,5},{6,7},{8,9},{10,11},{12,13},{14,15},{16,17},{18,... | collective-permute-start | bytes 20 | tf_op jit(solution)/shard_map/ppermute | solution.py:344
